TPU v7x, 512 devices: a whole 4x8x8 slice. The times are simulated.
512 devices in a mesh: blk: 32 (over z, y_lo, core), head: 16 (over y_hi, x).
Axes of the slice: x: 4, y: 8 (y_hi: 4, y_lo: 2; y = y_hi * 2 + y_lo), z: 8, core: 2. Of those that a mesh axis runs over, the one named last changes fastest.
Arguments:
- queries: bfloat16 [4096, 128, 192], P('blk', 'head'), may hold values from -8 to 8
- latent: bfloat16 [4096, 576], P(('blk', 'head')), may hold values from -8 to 8
- key_up_weight: bfloat16 [128, 128, 512], P('head'), may hold values from -0.5 to 0.5
- value_up_weight: bfloat16 [128, 512, 128], P('head'), may hold values from -0.25 to 0.25
- w_o: bfloat16 [16384, 3584], P('head', 'blk'), may hold values from -0.046875 to 0.046875
- block_order: int32 [64], replicated, may hold values from 0 to 63, each once
Outputs:
- attended: bfloat16 [4096, 3584], P(('blk', 'head'))
All inputs are finite; a program needn't handle non-finite values.
Results may differ from a plain program's by a relative error of at most 0.023.
Values may be sent and summed in bfloat16 or wider, within the bound.
A program may use at most 128 MiB of HBM per device.

v0:
```python
import jax
import jax.numpy as jnp
from jax import lax
from jax.sharding import PartitionSpec as P

PLAIN_QUERY_DIM = 128
ROTARY_WIDTH = 64
LATENT_WIDTH = 512
VALUE_WIDTH = 128
BLOCK_SPAN = 8


def from_behind(value, axis, steps):
    count = lax.axis_size(axis)
    pairs = [(source, (source + steps) % count) for source in range(count)]
    return lax.ppermute(value, axis, pairs)


def positions(order, device, half):
    pair = lax.dynamic_slice(order, (2 * device,), (2,))
    rows = jnp.arange(2 * half, dtype=jnp.int32)
    return jnp.where(rows < half, pair[0], pair[1]) * half + rows % half


def attend(state, q_here, q_pos, key_rows, key_pos):
    run_max, grand_total, accum = state
    scale = (PLAIN_QUERY_DIM + ROTARY_WIDTH) ** (-0.5)
    scores = jnp.einsum("thc,uc->thu", q_here, key_rows, preferred_element_type=jnp.float32) * scale
    visible = key_pos[None, None, :] <= q_pos[:, None, None]
    top = jnp.max(jnp.where(visible, scores, -1e30), axis=-1)
    new_max = jnp.maximum(run_max, top)
    shrink = jnp.exp(run_max - new_max)
    expo = jnp.where(visible, jnp.exp(scores - new_max[..., None]), 0.0)
    grand_total = grand_total * shrink + jnp.sum(expo, axis=-1)
    accum = accum * shrink[..., None] + jnp.einsum(
        "qnj,jy->qny",
        expo.astype(jnp.bfloat16),
        key_rows[:, :LATENT_WIDTH],
        preferred_element_type=jnp.float32,
    )
    return (new_max, grand_total, accum)


def shards(queries, latent, key_up_weight, value_up_weight, w_o, block_order):
    nblocks = lax.axis_size("blk")
    mine = lax.axis_index("blk")
    local_tokens = queries.shape[0]
    half = local_tokens // 2
    local_heads = queries.shape[1]
    q_lat = jnp.einsum(
        "thn,hnc->thc",
        queries[:, :, :PLAIN_QUERY_DIM],
        key_up_weight,
        preferred_element_type=jnp.float32,
    ).astype(jnp.bfloat16)
    q_full = jnp.concatenate([q_lat, queries[:, :, PLAIN_QUERY_DIM:]], axis=-1)
    q_pos = positions(block_order, mine, half)
    state = (
        jnp.full((local_tokens, local_heads), -1e30, jnp.float32),
        jnp.zeros((local_tokens, local_heads), jnp.float32),
        jnp.zeros((local_tokens, local_heads, LATENT_WIDTH), jnp.float32),
    )
    carried = lax.all_gather(latent, "head", axis=0, tiled=True)
    for step in range(BLOCK_SPAN):
        if step > 0:
            carried = from_behind(carried, "blk", 1)
        source = (mine - step) % nblocks
        key_pos = positions(block_order, source, half)
        state = attend(state, q_full, q_pos, carried, key_pos)
    context_rows = (state[2] / state[1][..., None]).astype(jnp.bfloat16)
    values = jnp.einsum(
        "thc,hcv->thv", context_rows, value_up_weight, preferred_element_type=jnp.float32
    ).astype(jnp.bfloat16)
    values = values.reshape(local_tokens, local_heads * VALUE_WIDTH)
    every_block = jnp.dot(
        lax.all_gather(values, "blk", axis=0, tiled=True), w_o, preferred_element_type=jnp.float32
    ).astype(jnp.bfloat16)
    term = lax.all_to_all(every_block, "blk", split_axis=0, concat_axis=1, tiled=True)
    term_wide = lax.optimization_barrier(term).astype(jnp.float32)
    summed = lax.psum_scatter(
        term_wide.astype(jnp.bfloat16), "head", scatter_dimension=0, tiled=True
    )
    return summed


def solution(mesh):
    placed = (
        P("blk", "head", None),
        P(("blk", "head"), None),
        P("head", None, None),
        P("head", None, None),
        P("head", "blk"),
        P(),
    )
    return jax.shard_map(
        shards, mesh=mesh, in_specs=placed, out_specs=P(("blk", "head"), None), check_vma=False
    )
```

profile of v0, /device:TPU:56, one launch (start us, length us, event | category | flops | bytes accessed | tf_op | source)
XLA Modules:
  0.0 367.9 jit_solution(2437745082473339560)
XLA Ops:
  6.5 38.8 %all_gather.6 = bf16[128,576]{1,0:T(8,128)(2,1)S(1)} all-gather(bf16[8,576]{1,0:T(8,128)(2,1)} %param.7), channel_id=1, replica_groups=mesh['blk'=32,'head'=16] {'head'}, dimensions={0}, use_global_device_ids=true | all-gather | bytes 156672 | tf_op jit(solution)/shard_map/all_gather | solution.py:63
  45.3 1.9 collective-permute-start
  47.4 1.1 fusion.94
  48.5 0.7 fusion.102
  49.1 0.9 slice.89
  50.0 1.5 fusion
  51.5 0.7 fusion.93
  52.2 1.2 multiply_add_fusion.9
  53.4 1.2 multiply_add_fusion.7
  54.6 1.3 multiply_add_fusion.8
  56.0 0.7 fusion.98
  56.6 1.3 multiply_add_fusion.4
  58.0 1.2 multiply_add_fusion.3
  59.2 0.7 fusion.96
  59.8 1.3 multiply_add_fusion.6
  61.2 1.2 multiply_add_fusion.5
  62.4 0.7 fusion.100
  63.1 1.3 multiply_add_fusion.2
  64.4 1.2 multiply_add_fusion.1
  65.6 0.2 broadcast_compare_fusion.7
  65.8 0.4 select_reduce_fusion.7
  66.2 5.1 %collective-permute-start.1 = (bf16[128,576]{1,0:T(8,128)(2,1)S(1)}, bf16[128,576]{1,0:T(8,128)(2,1)S(1)}, u32[]{:S(2)}, u32[]{:S(2)}) collective-permute-start(bf16[128,576]{1,0:T(8,128)(2,1)S(1)} %collective-permute-done), channel_id=1, source_target_pairs={{0,16},{16,32},{32,48},{48,64},{64,80},{80,96},{96,112},{112,128},... | collective-permute-start | bytes 442376 | tf_op jit(solution)/shard_map/ppermute | solution.py:16
  71.3 0.4 select_reduce_fusion.6
  71.7 1.2 collective-permute-done.1
  72.9 2.6 collective-permute-start.2
  75.5 0.4 select_reduce_fusion.5
  75.9 3.6 collective-permute-done.2
  79.5 3.5 collective-permute-start.3
  83.0 0.4 select_reduce_fusion.4
  83.4 2.7 collective-permute-done.3
  86.1 4.4 %collective-permute-start.4 = (bf16[128,576]{1,0:T(8,128)(2,1)S(1)}, bf16[128,576]{1,0:T(8,128)(2,1)S(1)}, u32[]{:S(2)}, u32[]{:S(2)}) collective-permute-start(bf16[128,576]{1,0:T(8,128)(2,1)S(1)} %collective-permute-done.3), channel_id=1, source_target_pairs={{0,16},{16,32},{32,48},{48,64},{64,80},{80,96},{96,112},{112,128},... | collective-permute-start | bytes 442376 | tf_op jit(solution)/shard_map/ppermute | solution.py:16
  90.5 0.4 select_reduce_fusion.3
  90.9 1.8 collective-permute-done.4
  92.8 5.3 %collective-permute-start.5 = (bf16[128,576]{1,0:T(8,128)(2,1)S(1)}, bf16[128,576]{1,0:T(8,128)(2,1)S(1)}, u32[]{:S(2)}, u32[]{:S(2)}) collective-permute-start(bf16[128,576]{1,0:T(8,128)(2,1)S(1)} %collective-permute-done.4), channel_id=1, source_target_pairs={{0,16},{16,32},{32,48},{48,64},{64,80},{80,96},{96,112},{112,128},... | collective-permute-start | bytes 442376 | tf_op jit(solution)/shard_map/ppermute | solution.py:16
  98.0 0.4 select_reduce_fusion.2
  98.4 3.1 collective-permute-done.5
  101.5 4.1 %collective-permute-start.6 = (bf16[128,576]{1,0:T(8,128)(2,1)S(1)}, bf16[128,576]{1,0:T(8,128)(2,1)S(1)}, u32[]{:S(2)}, u32[]{:S(2)}) collective-permute-start(bf16[128,576]{1,0:T(8,128)(2,1)S(1)} %collective-permute-done.5), channel_id=1, source_target_pairs={{0,16},{16,32},{32,48},{48,64},{64,80},{80,96},{96,112},{112,128},... | collective-permute-start | bytes 442376 | tf_op jit(solution)/shard_map/ppermute | solution.py:16
  105.6 0.4 select_reduce_fusion.1
  106.0 4.3 %collective-permute-done.6 = bf16[128,576]{1,0:T(8,128)(2,1)S(1)} collective-permute-done((bf16[128,576]{1,0:T(8,128)(2,1)S(1)}, bf16[128,576]{1,0:T(8,128)(2,1)S(1)}, u32[]{:S(2)}, u32[]{:S(2)}) %collective-permute-start.6) | collective-permute-done | bytes 147488 | tf_op jit(solution)/shard_map/ppermute | solution.py:16
  110.2 0.4 select_reduce_fusion
  110.6 0.7 fusion.91
  111.3 0.1 fusion.13
  111.4 0.5 fusion.43
  111.9 0.1 fusion.27
  112.0 0.1 fusion.25
  112.1 0.1 fusion.23
  112.2 0.1 fusion.21
  112.3 0.1 fusion.19
  112.5 0.1 fusion.17
  112.6 0.1 fusion.15
  112.7 0.7 multiply_add_fusion
  113.3 1.8 fusion.31
  115.2 1.8 fusion.33
  116.9 1.8 fusion.35
  118.8 1.8 fusion.37
  120.6 1.9 fusion.39
  122.5 1.8 fusion.41
  124.2 7.7 %fusion.3 = bf16[8,128,128]{1,2,0:T(8,128)(2,1)} fusion(bf16[8,512,128]{2,1,0:T(8,128)(2,1)} %param.9, f32[128,8,512]{2,0,1:T(8,128)} %fusion.31, f32[128,8,512]{2,0,1:T(8,128)} %fusion.33, f32[128,8,512]{2,0,1:T(8,128)} %fusion.35, f32[128,8,512]{2,0,1:T(8,128)} %fusion.37, f32[128,8,512]{2,0,1:T(8,128)} %fusion.39, f32[128,8,512]{2,0,1:T(8,128)} %fusion.41, ...), kind=kOutput, calls=%fused_computation.14 | convolution fusion | flops 277872640 | bytes 16703488 | tf_op jit(solution)/shard_map/thc,hcv->thv/dot_general | solution.py:71
  132.0 106.1 %all-gather.2.cloned.1.call-done = bf16[4096,1024]{0,1:T(8,128)(2,1)} async-done(((bf16[128,1024]{0,1:T(8,128)(2,1)}), bf16[4096,1024]{0,1:T(8,128)(2,1)}) %all-gather.2.cloned.1.call-update) | async-done | bytes 8388624 | tf_op jit(solution)/shard_map/all_gather | solution.py:76
  238.1 4.8 %fusion.1 = bf16[14,32,8,128]{3,2,1,0:T(8,128)(2,1)S(1)} fusion(bf16[1024,112]{0,1:T(8,128)(2,1)S(1)} %copy-done.2, bf16[4096,1024]{0,1:T(8,128)(2,1)} %all-gather.2.cloned.1.call-done), kind=kOutput, calls=%fused_computation.4 | convolution fusion | flops 939982848 | bytes 9535488 | tf_op jit(solution)/shard_map/dot_general | solution.py:75
  242.9 0.2 copy.79
  243.1 31.6 %all_to_all.19 = bf16[32,128,112]{1,2,0:T(8,128)(2,1)S(1)} all-to-all(bf16[32,128,112]{1,2,0:T(8,128)(2,1)S(1)} %bitcast.101), channel_id=1, replica_groups=mesh['blk'=32,'head'=16] {'blk'}, dimensions={0} | all-to-all | bytes 1835008 | tf_op jit(solution)/shard_map/all_to_all | solution.py:78
  274.7 1.3 copy.74
  276.0 85.0 %reduce-scatter.4.cloned.1.call-done = bf16[8,3584]{1,0:T(8,128)(2,1)} async-done(((bf16[128,3584]{1,0:T(8,128)(2,1)}), bf16[8,3584]{1,0:T(8,128)(2,1)}) %reduce-scatter.4.cloned.1.call-update) | async-done | bytes 57360 | tf_op jit(solution)/shard_map/reduce_scatter | solution.py:80
  (17 shorter events, 0.1 us)
Async XLA Ops:
  6.5 43.5 %copy-start = (bf16[8,128,512]{2,1,0:T(8,128)(2,1)S(1)}, bf16[8,128,512]{2,1,0:T(8,128)(2,1)}, u32[]{:S(2)}) copy-start(bf16[8,128,512]{2,1,0:T(8,128)(2,1)} %param.8) | copy-start | bytes 3145732
  6.5 231.6 %all-gather.2.cloned.1.call-start = ((), (), s32[]{:S(2)}) async-start(), calls=%async_computation.2 | async-start | bytes 8650752 | tf_op jit(solution)/shard_map/all_gather | solution.py:76
  45.3 20.9 %collective-permute-start = (bf16[128,576]{1,0:T(8,128)(2,1)S(1)}, bf16[128,576]{1,0:T(8,128)(2,1)S(1)}, u32[]{:S(2)}, u32[]{:S(2)}) collective-permute-start(bf16[128,576]{1,0:T(8,128)(2,1)S(1)} %all_gather.6), channel_id=1, source_target_pairs={{0,16},{16,32},{32,48},{48,64},{64,80},{80,96},{96,112},{112,128},... | collective-permute-start | bytes 442376 | tf_op jit(solution)/shard_map/ppermute | solution.py:16
  66.2 9.6 %copy-start.3 = (bf16[128,576]{1,0:T(8,128)(2,1)}, bf16[128,576]{1,0:T(8,128)(2,1)S(1)}, u32[]{:S(2)}) copy-start(bf16[128,576]{1,0:T(8,128)(2,1)S(1)} %collective-permute-done) | copy-start | bytes 442372
  66.2 6.6 %collective-permute-start.1 = (bf16[128,576]{1,0:T(8,128)(2,1)S(1)}, bf16[128,576]{1,0:T(8,128)(2,1)S(1)}, u32[]{:S(2)}, u32[]{:S(2)}) collective-permute-start(bf16[128,576]{1,0:T(8,128)(2,1)S(1)} %collective-permute-done), channel_id=1, source_target_pairs={{0,16},{16,32},{32,48},{48,64},{64,80},{80,96},{96,112},{112,128},... | collective-permute-start | bytes 442376 | tf_op jit(solution)/shard_map/ppermute | solution.py:16
  72.9 6.6 %collective-permute-start.2 = (bf16[128,576]{1,0:T(8,128)(2,1)S(1)}, bf16[128,576]{1,0:T(8,128)(2,1)S(1)}, u32[]{:S(2)}, u32[]{:S(2)}) collective-permute-start(bf16[128,576]{1,0:T(8,128)(2,1)S(1)} %collective-permute-done.1), channel_id=1, source_target_pairs={{0,16},{16,32},{32,48},{48,64},{64,80},{80,96},{96,112},{112,128},... | collective-permute-start | bytes 442376 | tf_op jit(solution)/shard_map/ppermute | solution.py:16
  79.5 6.6 %collective-permute-start.3 = (bf16[128,576]{1,0:T(8,128)(2,1)S(1)}, bf16[128,576]{1,0:T(8,128)(2,1)S(1)}, u32[]{:S(2)}, u32[]{:S(2)}) collective-permute-start(bf16[128,576]{1,0:T(8,128)(2,1)S(1)} %collective-permute-done.2), channel_id=1, source_target_pairs={{0,16},{16,32},{32,48},{48,64},{64,80},{80,96},{96,112},{112,128},... | collective-permute-start | bytes 442376 | tf_op jit(solution)/shard_map/ppermute | solution.py:16
  86.1 6.6 %collective-permute-start.4 = (bf16[128,576]{1,0:T(8,128)(2,1)S(1)}, bf16[128,576]{1,0:T(8,128)(2,1)S(1)}, u32[]{:S(2)}, u32[]{:S(2)}) collective-permute-start(bf16[128,576]{1,0:T(8,128)(2,1)S(1)} %collective-permute-done.3), channel_id=1, source_target_pairs={{0,16},{16,32},{32,48},{48,64},{64,80},{80,96},{96,112},{112,128},... | collective-permute-start | bytes 442376 | tf_op jit(solution)/shard_map/ppermute | solution.py:16
  92.8 8.7 %collective-permute-start.5 = (bf16[128,576]{1,0:T(8,128)(2,1)S(1)}, bf16[128,576]{1,0:T(8,128)(2,1)S(1)}, u32[]{:S(2)}, u32[]{:S(2)}) collective-permute-start(bf16[128,576]{1,0:T(8,128)(2,1)S(1)} %collective-permute-done.4), channel_id=1, source_target_pairs={{0,16},{16,32},{32,48},{48,64},{64,80},{80,96},{96,112},{112,128},... | collective-permute-start | bytes 442376 | tf_op jit(solution)/shard_map/ppermute | solution.py:16
  101.5 8.7 %collective-permute-start.6 = (bf16[128,576]{1,0:T(8,128)(2,1)S(1)}, bf16[128,576]{1,0:T(8,128)(2,1)S(1)}, u32[]{:S(2)}, u32[]{:S(2)}) collective-permute-start(bf16[128,576]{1,0:T(8,128)(2,1)S(1)} %collective-permute-done.5), channel_id=1, source_target_pairs={{0,16},{16,32},{32,48},{48,64},{64,80},{80,96},{96,112},{112,128},... | collective-permute-start | bytes 442376 | tf_op jit(solution)/shard_map/ppermute | solution.py:16
  110.6 1.5 copy-start.1
  111.3 1.4 copy-start.5
  118.8 3.7 %copy-start.4 = (bf16[128,576]{1,0:T(8,128)(2,1)S(1)}, bf16[128,576]{1,0:T(8,128)(2,1)}, u32[]{:S(2)}) copy-start(bf16[128,576]{1,0:T(8,128)(2,1)} %copy-done.3) | copy-start | bytes 442372
  124.2 113.9 %copy-start.2 = (bf16[1024,112]{0,1:T(8,128)(2,1)S(1)}, bf16[1024,112]{0,1:T(8,128)(2,1)}, u32[]{:S(2)}) copy-start(bf16[1024,112]{0,1:T(8,128)(2,1)} %param.10) | copy-start | bytes 688132
  132.0 229.1 %reduce-scatter.4.cloned.1.call-start = ((), (), s32[]{:S(2)}) async-start(), calls=%async_computation.3 | async-start | bytes 974848 | tf_op jit(solution)/shard_map/reduce_scatter | solution.py:80
Sparse Core Ops, SparseCore 0:
  132.1 105.9 all-gather.1
  276.2 84.8 reduce-scatter.3
where the time goes:
time: 370 us; the launch traced here: 368 us
  waiting for transfers between devices  208 us (56%)
  blocking collectives  70.4 us (19%)
  matrix products  28.4 us (8%)
  starting transfers between devices  26.8 us (7%)
  between operations  13.9 us (4%)
  other arithmetic  13.8 us (4%)
  local copies, waits for them, and re-layouts  6.8 us (2%)
    all_gather x1, waiting for transfers between devices, shards(): lax.all_gather(values, 'blk', axis=0, tiled=True)  106 us
    reduce_scatter x1, waiting for transfers between devices, shards(): lax.psum_scatter(term_wide.astype(jnp.bfloat16), 'head', scatter_dimensio...  85 us
    all_gather x1, blocking collectives, shards(): carried = lax.all_gather(latent, 'head', axis=0, tiled=True)  38.8 us
    all_to_all x1, blocking collectives, shards(): lax.all_to_all(every_block, 'blk', split_axis=0, concat_axis=1, tiled=True)  31.6 us
    ppermute x7, starting transfers between devices, from_behind(): return lax.ppermute(value, axis, pairs)  26.8 us
    ppermute x7, waiting for transfers between devices, from_behind(): return lax.ppermute(value, axis, pairs)  16.7 us
    add x9, other arithmetic, positions(): return jnp.where(rows < half, pair[0], pair[1]) * half + rows % half  11.4 us
    dot_general x7, matrix products, attend(): jnp.einsum('qnj,jy->qny', expo.astype(jnp.bfloat16), key_rows[:, :LATENT_...  11.4 us
  transfers between devices with their start and end apart: 9, of which 8 were waited for; matrix products, arithmetic and copies ran while one was open for 6% of the time, Pallas kernels for 0%

commit v1 on v0

v1 whole, which is shorter than its diff:
```python
import functools
import math

import jax
import jax.numpy as jnp
from jax import lax
from jax.experimental import pallas as pl
from jax.experimental.pallas import tpu as pltpu
from jax.sharding import PartitionSpec as P

NOPE = 128
ROT = 64
LAT = 512
WIDTH = LAT + ROT
VAL = 128
HEADS = 8
TOKENS = 128
HALF = 64
SPAN = 8
NBLK = 32
COLS = 112
MINE = 1792
WIDE = ((0, 512), (1024, 384))
GAIN = (NOPE + ROT) ** (-0.5) * math.log2(math.e)
HIDDEN = -1e30
NT = (((1,), (1,)), ((), ()))
F32 = jnp.float32
BF16 = jnp.bfloat16


def nt_dot(a, b):
    return lax.dot_general(a, b, NT, preferred_element_type=F32)


def remote(src, dst, send, recv, device):
    return pltpu.make_async_remote_copy(
        src_ref=src, dst_ref=dst, send_sem=send, recv_sem=recv,
        device_id=device, device_id_type=pl.DeviceIdType.MESH,
    )


def kernel(
    order, latent, q_hbm, ku_hbm, vu_hbm, wo_hbm, out,
    q_raw, q_plain, q_rot, ku, vu, wo, q_full, bias, pack, keys, wt, vals,
    top, total, accum, terms_a, terms_b, got_a, got_b, part_a, part_b, fin_a, fin_b,
    load_sem, ps, pr, lzs, lzr, lcs, lcr, lys, lyr, lds, ldr,
    wps, wpr, wms, wmr, wcs, wcr, vs, vr, xs, xr, yss, ysr, yos, yor,
):
    b = lax.axis_index("blk")
    h = lax.axis_index("head")
    z, c = b // 4, b % 4
    lo, core = c // 2, c % 2
    hi, x = h // 4, h % 4
    up = (b + 4) % NBLK
    down = (b + NBLK - 4) % NBLK
    mate = b + 1 - 2 * core
    side = b + 2 - 4 * lo
    c_mate = c + 1 - 2 * core
    c_side = c + 2 - 4 * lo
    c_diag = c_side + 1 - 2 * core

    loads = [
        pltpu.make_async_copy(src, dst, load_sem.at[i])
        for i, (src, dst) in enumerate(((wo_hbm, wo), (q_hbm, q_raw), (ku_hbm, ku), (vu_hbm, vu)))
    ]
    for load in loads:
        load.start()

    rows = latent[...].astype(F32)
    second = jnp.concatenate([rows[:, 384:], jnp.zeros((8, 192), F32)], axis=1)
    pack[h] = jnp.concatenate([rows[:, :384], second], axis=0).astype(BF16)

    barrier = pltpu.get_barrier_semaphore()

    def greet(device):
        pl.semaphore_signal(barrier, inc=1, device_id=device, device_id_type=pl.DeviceIdType.MESH)

    @pl.loop(1, 16)
    def _(i):
        greet({"head": (h + i) % 16})

    @pl.loop(0, 4)
    def _(i):
        greet({"blk": side, "head": (hi + i) % 4 * 4 + x})

    greet({"blk": up})
    greet({"blk": down})
    greet({"blk": mate})
    pl.semaphore_wait(barrier, 22)

    def own_rows(i):
        return remote(pack.at[h], pack.at[h], ps.at[i], pr.at[i], {"head": (h + i) % 16})

    @pl.loop(1, 16)
    def _(i):
        own_rows(i).start()

    def shard(zz, cc):
        return wt.at[pl.ds(pl.multiple_of((zz * 2 + cc) * COLS, 16), COLS)]

    def w_plus(k):
        ref = shard((z + 8 - k) % 8, core)
        return remote(ref, ref, wps.at[k], wpr.at[k], {"blk": up})

    def w_minus(k):
        ref = shard((z + k) % 8, core)
        return remote(ref, ref, wms.at[k], wmr.at[k], {"blk": down})

    def w_core(k):
        zz = (z + 8 - k) % 8 if k < 4 else (z + k - 3) % 8
        ref = shard(zz, core)
        return remote(ref, ref, wcs.at[k], wcr.at[k], {"blk": mate})

    def w_core_in(k):
        zz = (z + 8 - k) % 8 if k < 4 else (z + k - 3) % 8
        ref = shard(zz, 1 - core)
        return remote(ref, ref, wcs.at[k], wcr.at[k], {"blk": mate})

    def w_plus_in(k):
        ref = shard((z + 7 - k) % 8, core)
        return remote(ref, ref, wps.at[k], wpr.at[k], {"blk": up})

    def w_minus_in(k):
        ref = shard((z + 1 + k) % 8, core)
        return remote(ref, ref, wms.at[k], wmr.at[k], {"blk": down})

    loads[0].wait()
    r = lax.broadcasted_iota(jnp.int32, (COLS, COLS), 0)
    s = lax.broadcasted_iota(jnp.int32, (COLS, COLS), 1)
    eye = jnp.where(r == s, 1.0, 0.0).astype(BF16)
    wt[pl.ds(pl.multiple_of((z * 2 + core) * COLS, 16), COLS), :] = nt_dot(eye, wo[...]).astype(BF16)
    w_plus(0).start()
    w_minus(0).start()
    w_core(0).start()

    loads[1].wait()
    q_plain[...] = q_raw[:, :, :NOPE].astype(F32).reshape(TOKENS * HEADS, NOPE)
    q_rot[:, :ROT] = q_raw[:, :, NOPE:].astype(F32).reshape(TOKENS * HEADS, ROT)
    loads[2].wait()
    for n in range(HEADS):
        plain = q_plain[pl.ds(n, TOKENS, stride=HEADS), :].astype(BF16)
        q_full[n * TOKENS:(n + 1) * TOKENS, :LAT] = jnp.dot(
            plain, ku[n], preferred_element_type=F32
        ).astype(BF16)
        q_full[n * TOKENS:(n + 1) * TOKENS, LAT:] = q_rot[pl.ds(n, TOKENS, stride=HEADS), :][:, :ROT].astype(BF16)

    row = lax.broadcasted_iota(jnp.int32, (TOKENS, TOKENS), 0)
    col = lax.broadcasted_iota(jnp.int32, (TOKENS, TOKENS), 1)
    q_pos = jnp.where(row < HALF, order[2 * b], order[2 * b + 1]) * HALF + row % HALF
    for n in range(SPAN):
        src = (b + NBLK - 7 + n) % NBLK
        k_pos = jnp.where(col < HALF, order[2 * src], order[2 * src + 1]) * HALF + col % HALF
        bias[:, n * TOKENS:(n + 1) * TOKENS] = jnp.where(k_pos <= q_pos, 0.0, HIDDEN)

    @pl.loop(1, 16)
    def _(i):
        ref = pack.at[(h + 16 - i) % 16]
        remote(ref, ref, ps.at[i], pr.at[i], {"head": (h + i) % 16}).wait_recv()

    def slot(plane, cc):
        return keys.at[pl.ds(pl.multiple_of((8 - 4 * plane + cc) * TOKENS, TOKENS), TOKENS)]

    gathered = pack[...].astype(F32)
    base = pl.multiple_of((8 + c) * TOKENS, TOKENS)
    keys[pl.ds(base, TOKENS), :384] = gathered[:, :8, :].reshape(TOKENS, 384).astype(BF16)
    keys[pl.ds(base, TOKENS), 384:] = gathered[:, 8:, :192].reshape(TOKENS, 192).astype(BF16)

    def l_up(k):
        return remote(slot(k, c), slot(k + 1, c), lzs.at[k], lzr.at[k], {"blk": up})

    def l_up_in(k):
        return remote(slot(k + 1, c), slot(k + 1, c), lzs.at[k], lzr.at[k], {"blk": up})

    def l_core(p):
        return remote(slot(p, c), slot(p, c), lcs.at[p], lcr.at[p], {"blk": mate})

    def l_core_in(p):
        return remote(slot(p, c_mate), slot(p, c_mate), lcs.at[p], lcr.at[p], {"blk": mate})

    def l_side(j):
        ref = slot(j + lo, c)
        return remote(ref, ref, lys.at[j], lyr.at[j], {"blk": side})

    def l_side_in(j):
        ref = slot(j + 1 - lo, c_side)
        return remote(ref, ref, lys.at[j], lyr.at[j], {"blk": side})

    def l_diag(j):
        ref = slot(j + 1 - lo, c_side)
        return remote(ref, ref, lds.at[j], ldr.at[j], {"blk": mate})

    def l_diag_in(j):
        ref = slot(j + 1 - lo, c_diag)
        return remote(ref, ref, lds.at[j], ldr.at[j], {"blk": mate})

    def w_step_plus(k):
        w_plus_in(k - 1).wait_recv()
        if k < 3:
            w_plus(k).start()
        w_core(k).start()

    def w_step_minus(k):
        w_minus_in(k - 1).wait_recv()
        if k < 4:
            w_minus(k).start()
        w_core(3 + k).start()

    l_up(0).start()

    @pl.when(lo == 0)
    def _():
        l_side(0).start()

    l_core(0).start()

    w_step_minus(1)
    l_up_in(0).wait_recv()
    l_up(1).start()

    @pl.when(lo == 0)
    def _():
        l_side(1).start()

    @pl.when(lo == 1)
    def _():
        l_side(0).start()

    l_core(1).start()
    w_step_plus(1)
    l_side_in(0).wait_recv()
    l_diag(0).start()
    l_core_in(0).wait_recv()
    l_core_in(1).wait_recv()
    l_diag_in(0).wait_recv()

    def scores(i, start, first):
        q = q_full[pl.ds(pl.multiple_of(i * 256, 256), 256), :]
        k = keys[pl.ds(pl.multiple_of(start, TOKENS), 512), :]
        sc = nt_dot(q, k).reshape(2, TOKENS, 512) + bias[:, first:first + 512][None]
        return sc.reshape(256, 512), k

    def near(i):
        at = pl.ds(pl.multiple_of(i * 256, 256), 256)
        sc, k = scores(i, (c + 5) * TOKENS, 512)
        m = jnp.max(sc, axis=1, keepdims=True)
        e = jnp.exp2((sc - m) * GAIN)
        top[at, :] = jnp.broadcast_to(m, (256, 128))
        total[at, :] = jnp.broadcast_to(jnp.sum(e, axis=1, keepdims=True), (256, 128))
        accum[at, :] = jnp.dot(e.astype(BF16), k[:, :LAT], preferred_element_type=F32)

    def v_out(i):
        ref = vals.at[lo, :, pl.ds(pl.multiple_of(i * 256, 256), 256)]
        return remote(ref, ref, vs.at[i], vr.at[i], {"blk": side})

    def v_in(i):
        ref = vals.at[1 - lo, :, pl.ds(pl.multiple_of(i * 256, 256), 256)]
        return remote(ref, ref, vs.at[i], vr.at[i], {"blk": side})

    def far(i):
        at = pl.ds(pl.multiple_of(i * 256, 256), 256)
        sc, k = scores(i, (c + 1) * TOKENS, 0)
        old = top[at, :][:, :1]
        m = jnp.maximum(old, jnp.max(sc, axis=1, keepdims=True))
        e = jnp.exp2((sc - m) * GAIN)
        shrink = jnp.exp2((old - m) * GAIN)
        tot = total[at, :][:, :1] * shrink + jnp.sum(e, axis=1, keepdims=True)
        acc = accum[at, :] * shrink + jnp.dot(e.astype(BF16), k[:, :LAT], preferred_element_type=F32)
        ctx = (acc * (1.0 / tot)).astype(BF16)
        for n in range(2):
            v = jnp.dot(ctx[n * TOKENS:(n + 1) * TOKENS], vu[2 * i + n], preferred_element_type=F32)
            vals[lo, :, pl.ds(pl.multiple_of(i * 256 + n * VAL, VAL), VAL)] = v.astype(BF16)
        v_out(i).start()

    pl.loop(0, 2)(near)
    w_step_minus(2)
    w_step_plus(2)
    l_up_in(1).wait_recv()

    @pl.when(lo == 1)
    def _():
        l_side(1).start()

    l_core(2).start()
    pl.loop(2, 4)(near)
    l_side_in(1).wait_recv()
    l_diag(1).start()
    w_step_minus(3)
    w_step_plus(3)
    loads[3].wait()
    l_core_in(2).wait_recv()
    l_diag_in(1).wait_recv()
    pl.loop(0, 2)(far)
    w_step_minus(4)
    pl.loop(2, 4)(far)
    for k in range(8):
        w_core_in(k).wait_recv()

    def x_out(y, n, step, d):
        terms, got = ((terms_a, got_a), (terms_b, got_b))[n]
        xd = (x + d) % 4
        return remote(
            terms.at[y, :, xd], got.at[y, d - 1],
            xs.at[n, step, d - 1], xr.at[n, step, d - 1], {"head": hi * 4 + xd},
        )

    def project(y, n, step):
        first, width = WIDE[n]
        terms = (terms_a, terms_b)[n]
        t = nt_dot(vals[y], wt[first:first + 2 * width, :])
        left = t[:, :width].reshape(16, 8, width)
        right = t[:, width:].reshape(16, 8, width)
        both = jnp.concatenate([left, right], axis=1).astype(BF16)
        terms[y] = both.reshape(4, 4, 16, width)
        for d in (2, 1, 3):
            x_out(y, n, step, d).start()

    def y_same(n, e):
        part, fin = ((part_a, fin_a), (part_b, fin_b))[n]
        yd = (hi + e) % 4
        return remote(
            part.at[lo, yd], fin.at[0, e], yss.at[n, e], ysr.at[n, e], {"head": yd * 4 + x}
        )

    def y_other(n, e):
        part, fin = ((part_a, fin_a), (part_b, fin_b))[n]
        yd = (hi + e) % 4
        return remote(
            part.at[1 - lo, yd], fin.at[1, e], yos.at[n, e], yor.at[n, e],
            {"blk": side, "head": yd * 4 + x},
        )

    def combine(y, n, step):
        terms, got, part = ((terms_a, got_a, part_a), (terms_b, got_b, part_b))[n]
        for d in (1, 2, 3):
            x_out(y, n, step, d).wait_recv()
        t = terms[y, :, x].astype(F32)
        for d in range(3):
            t = t + got[y, d].astype(F32)
        part[y] = t.astype(BF16)

    for n in range(2):
        project(lo, n, 0)
    for i in range(4):
        v_in(i).wait_recv()
    for n in range(2):
        project(1 - lo, n, 1)
    for n in range(2):
        combine(lo, n, 0)
        for e in (2, 1, 3):
            y_same(n, e).start()
    for n in range(2):
        combine(1 - lo, n, 1)
        for e in (2, 1, 3, 0):
            y_other(n, e).start()
    for n, (first, width) in enumerate(WIDE):
        part, fin = ((part_a, fin_a), (part_b, fin_b))[n]
        same = part[lo, hi].astype(F32)
        for e in (1, 2, 3):
            y_same(n, e).wait_recv()
            same = same + fin[0, e].astype(F32)
        y_other(n, 0).wait_recv()
        other = fin[1, 0].astype(F32)
        for e in (1, 2, 3):
            y_other(n, e).wait_recv()
            other = other + fin[1, e].astype(F32)
        for y, v in ((lo, same), (1 - lo, other)):
            out[y, :, first:first + width] = v[:8]
            out[y, :, first + width:first + 2 * width] = v[8:]

    @pl.loop(1, 16)
    def _(i):
        own_rows(i).wait_send()

    for k in range(2):
        l_up(k).wait_send()
        l_side(k).wait_send()
        l_diag(k).wait_send()
    for k in range(3):
        l_core(k).wait_send()
        w_plus(k).wait_send()
    for k in range(4):
        w_minus(k).wait_send()
        v_out(k).wait_send()
    for k in range(8):
        w_core(k).wait_send()
    for n in range(2):
        for d in (1, 2, 3):
            x_out(lo, n, 0, d).wait_send()
            x_out(1 - lo, n, 1, d).wait_send()
            y_same(n, d).wait_send()
        for e in range(4):
            y_other(n, e).wait_send()


def shards(queries, latent, key_up_weight, value_up_weight, w_o, block_order):
    vmem = pl.BlockSpec(memory_space=pltpu.VMEM)
    anywhere = pl.BlockSpec(memory_space=pl.ANY)
    dma = pltpu.SemaphoreType.DMA
    rows = TOKENS * HEADS
    scratch = [
        pltpu.VMEM((TOKENS, HEADS, NOPE + ROT), BF16),
        pltpu.VMEM((rows, 128), F32),
        pltpu.VMEM((rows, 128), F32),
        pltpu.VMEM((HEADS, NOPE, LAT), BF16),
        pltpu.VMEM((HEADS, LAT, VAL), BF16),
        pltpu.VMEM((rows, COLS), BF16),
        pltpu.VMEM((rows, WIDTH), BF16),
        pltpu.VMEM((TOKENS, SPAN * TOKENS), F32),
        pltpu.VMEM((16, 16, 384), BF16),
        pltpu.VMEM((12 * TOKENS, WIDTH), BF16),
        pltpu.VMEM((MINE, HEADS * VAL), BF16),
        pltpu.VMEM((2, TOKENS, HEADS * VAL), BF16),
        pltpu.VMEM((rows, 128), F32),
        pltpu.VMEM((rows, 128), F32),
        pltpu.VMEM((rows, LAT), F32),
        pltpu.VMEM((2, 4, 4, 16, 512), BF16),
        pltpu.VMEM((2, 4, 4, 16, 384), BF16),
        pltpu.VMEM((2, 3, 4, 16, 512), BF16),
        pltpu.VMEM((2, 3, 4, 16, 384), BF16),
        pltpu.VMEM((2, 4, 16, 512), BF16),
        pltpu.VMEM((2, 4, 16, 384), BF16),
        pltpu.VMEM((2, 4, 16, 512), BF16),
        pltpu.VMEM((2, 4, 16, 384), BF16),
        dma((4,)),
        dma((16,)), dma((16,)),
        dma((2,)), dma((2,)),
        dma((3,)), dma((3,)),
        dma((2,)), dma((2,)),
        dma((2,)), dma((2,)),
        dma((3,)), dma((3,)),
        dma((4,)), dma((4,)),
        dma((8,)), dma((8,)),
        dma((4,)), dma((4,)),
        dma((2, 2, 3)), dma((2, 2, 3)),
        dma((2, 4)), dma((2, 4)),
        dma((2, 4)), dma((2, 4)),
    ]
    summed = pl.pallas_call(
        kernel,
        out_shape=jax.ShapeDtypeStruct((2, 8, MINE), F32),
        in_specs=[pl.BlockSpec(memory_space=pltpu.SMEM), vmem] + [anywhere] * 4,
        out_specs=vmem,
        scratch_shapes=scratch,
        compiler_params=pltpu.CompilerParams(
            collective_id=0, has_side_effects=True, vmem_limit_bytes=48 * 1024 * 1024
        ),
        cost_estimate=pl.CostEstimate(flops=3_500_000_000, bytes_accessed=3_000_000, transcendentals=1_048_576),
    )(block_order, latent, queries, key_up_weight, value_up_weight, w_o)
    return summed.reshape(2, 8, 8, 2 * COLS).transpose(1, 2, 0, 3).reshape(8, 32 * COLS).astype(BF16)


def solution(mesh):
    placed = (
        P("blk", "head", None),
        P(("blk", "head"), None),
        P("head", None, None),
        P("head", None, None),
        P("head", "blk"),
        P(),
    )
    return jax.shard_map(
        shards, mesh=mesh, in_specs=placed, out_specs=P(("blk", "head"), None), check_vma=False
    )
```

time: 370 us -> 74.1 us (0.20)
  the two profiles are of different devices: /device:TPU:56 before, /device:TPU:8 now
where the time goes in v1:
time: 74.1 us; the launch traced here: 73.9 us
  Pallas kernels  69 us (93%)
  local copies, waits for them, and re-layouts  4.79 us (6%)
    pallas_call x1, Pallas kernels, shards(): pl.pallas_call(kernel, out_shape=jax.ShapeDtypeStruct((2, 8, MINE), F32),...  69 us
    unnamed x10, local copies, waits for them, and re-layouts  3.83 us

profile of v1, /device:TPU:8, one launch (start us, length us, event | category | flops | bytes accessed | tf_op | source)
XLA Modules:
  0.0 73.9 jit_solution(12255084861130363407)
XLA Ops:
  0.0 0.0 copy-start
  0.0 1.2 %copy.8.wo_hbm = bf16[1024,112]{1,0:T(8,128)(2,1)S(1)} copy(bf16[1024,112]{0,1:T(8,128)(2,1)} %param.10) | data formatting | bytes 458752 | tf_op args[4]
  1.2 0.0 copy-start.2
  1.2 0.0 copy-start.3
  1.2 1.4 %copy.7.q_hbm = bf16[128,8,192]{2,1,0:T(8,128)(2,1)S(1)} copy(bf16[128,8,192]{0,2,1:T(8,128)(2,1)} %param.6) | data formatting | bytes 786432 | tf_op args[0]
  2.6 0.0 copy-done
  2.6 0.0 copy-done.2
  2.7 0.0 copy-done.3
  2.7 0.0 copy-start.1
  2.7 1.2 %copy-done.1 = bf16[8,512,128]{2,1,0:T(8,128)(2,1)S(1)} copy-done((bf16[8,512,128]{2,1,0:T(8,128)(2,1)S(1)}, bf16[8,512,128]{2,1,0:T(8,128)(2,1)}, u32[]{:S(2)}) %copy-start.1) | copy-done | bytes 1048600
  3.9 69.0 %shard_map.64 = f32[2,8,1792]{2,1,0:T(8,128)S(1)} custom-call(s32[64]{0:T(128)S(1)} %copy-done.3, bf16[8,576]{1,0:T(8,128)(2,1)S(1)} %copy-done.2, bf16[128,8,192]{2,1,0:T(8,128)(2,1)S(1)} %copy.7.q_hbm, bf16[8,128,512]{2,1,0:T(8,128)(2,1)S(1)} %copy-done, bf16[8,512,128]{2,1,0:T(8,128)(2,1)S(1)} %copy-done.1, bf16[1024,112]{1,0:T(8,128)(2,1)S(1)} %copy.8.wo_hbm), custom_call_target="tpu_custom_call" | custom-call | flops 3500000000 | bytes 3000000 | tf_op jit(solution)/shard_map/pallas_call | solution.py:438
  72.9 0.1 convert_element_type.13
  73.0 0.1 copy.9
  73.1 0.8 %convert_element_type.15 = bf16[8,3584]{1,0:T(8,128)(2,1)} reshape(bf16[8,8,2,224]{3,2,1,0:T(2,128)(2,1)S(1)} %copy.9) | data formatting | bytes 114688 | tf_op jit(solution)/shard_map/convert_element_type | solution.py:449
  (1 shorter events, 0.0 us)
Async XLA Ops:
  0.0 2.6 %copy-start = (bf16[8,128,512]{2,1,0:T(8,128)(2,1)S(1)}, bf16[8,128,512]{2,1,0:T(8,128)(2,1)}, u32[]{:S(2)}) copy-start(bf16[8,128,512]{2,1,0:T(8,128)(2,1)} %ku_hbm.1) | copy-start | bytes 3145732
  1.2 1.4 %copy-start.2 = (bf16[8,576]{1,0:T(8,128)(2,1)S(1)}, bf16[8,576]{1,0:T(8,128)(2,1)}, u32[]{:S(2)}) copy-start(bf16[8,576]{1,0:T(8,128)(2,1)} %latent.1) | copy-start | bytes 27652
  1.2 1.4 %copy-start.3 = (s32[64]{0:T(128)S(1)}, s32[64]{0:T(128)}, u32[]{:S(2)}) copy-start(s32[64]{0:T(128)} %order.1) | copy-start | bytes 772
  2.7 1.2 %copy-start.1 = (bf16[8,512,128]{2,1,0:T(8,128)(2,1)S(1)}, bf16[8,512,128]{2,1,0:T(8,128)(2,1)}, u32[]{:S(2)}) copy-start(bf16[8,512,128]{2,1,0:T(8,128)(2,1)} %vu_hbm.1) | copy-start | bytes 3145732

commit v2 on v1

--- a/solution.py
+++ b/solution.py
@@ -41,8 +41,8 @@
 
 def kernel(
     order, latent, q_hbm, ku_hbm, vu_hbm, wo_hbm, out,
-    q_raw, q_plain, q_rot, ku, vu, wo, q_full, bias, pack, keys, wt, vals,
-    top, total, accum, terms_a, terms_b, got_a, got_b, part_a, part_b, fin_a, fin_b,
+    q_raw, ku, vu, q_full, bias, pack, keys, wt, vals,
+    top, total, accum, terms_a, terms_b, got_a, got_b, relay_a, relay_b, part_a, part_b, fin_a, fin_b,
     load_sem, ps, pr, lzs, lzr, lcs, lcr, lys, lyr, lds, ldr,
     wps, wpr, wms, wmr, wcs, wcr, vs, vr, xs, xr, yss, ysr, yos, yor,
 ):
@@ -61,9 +61,11 @@
 
     loads = [
         pltpu.make_async_copy(src, dst, load_sem.at[i])
-        for i, (src, dst) in enumerate(((wo_hbm, wo), (q_hbm, q_raw), (ku_hbm, ku), (vu_hbm, vu)))
+        for i, (src, dst) in enumerate(((q_hbm, q_raw), (ku_hbm, ku), (vu_hbm, vu)))
     ]
-    for load in loads:
+    mine = wt.at[pl.ds(pl.multiple_of((z * 2 + core) * COLS, 16), COLS)]
+    loads.append(pltpu.make_async_copy(wo_hbm, mine, load_sem.at[3]))
+    for load in loads[3:] + loads[:3]:
         load.start()
 
     rows = latent[...].astype(F32)
@@ -124,25 +126,19 @@
         ref = shard((z + 1 + k) % 8, core)
         return remote(ref, ref, wms.at[k], wmr.at[k], {"blk": down})
 
-    loads[0].wait()
-    r = lax.broadcasted_iota(jnp.int32, (COLS, COLS), 0)
-    s = lax.broadcasted_iota(jnp.int32, (COLS, COLS), 1)
-    eye = jnp.where(r == s, 1.0, 0.0).astype(BF16)
-    wt[pl.ds(pl.multiple_of((z * 2 + core) * COLS, 16), COLS), :] = nt_dot(eye, wo[...]).astype(BF16)
+    loads[3].wait()
     w_plus(0).start()
     w_minus(0).start()
     w_core(0).start()
 
+    loads[0].wait()
     loads[1].wait()
-    q_plain[...] = q_raw[:, :, :NOPE].astype(F32).reshape(TOKENS * HEADS, NOPE)
-    q_rot[:, :ROT] = q_raw[:, :, NOPE:].astype(F32).reshape(TOKENS * HEADS, ROT)
-    loads[2].wait()
     for n in range(HEADS):
-        plain = q_plain[pl.ds(n, TOKENS, stride=HEADS), :].astype(BF16)
-        q_full[n * TOKENS:(n + 1) * TOKENS, :LAT] = jnp.dot(
-            plain, ku[n], preferred_element_type=F32
+        at = slice(n * TOKENS, (n + 1) * TOKENS)
+        q_full[at, :LAT] = lax.dot_general(
+            q_raw[n, :NOPE, :], ku[n], (((0,), (0,)), ((), ())), preferred_element_type=F32
         ).astype(BF16)
-        q_full[n * TOKENS:(n + 1) * TOKENS, LAT:] = q_rot[pl.ds(n, TOKENS, stride=HEADS), :][:, :ROT].astype(BF16)
+        q_full[at, LAT:] = q_raw[n, NOPE:, :].astype(F32).T.astype(BF16)
 
     row = lax.broadcasted_iota(jnp.int32, (TOKENS, TOKENS), 0)
     col = lax.broadcasted_iota(jnp.int32, (TOKENS, TOKENS), 1)
@@ -286,7 +282,7 @@
     l_diag(1).start()
     w_step_minus(3)
     w_step_plus(3)
-    loads[3].wait()
+    loads[2].wait()
     l_core_in(2).wait_recv()
     l_diag_in(1).wait_recv()
     pl.loop(0, 2)(far)
@@ -295,13 +291,16 @@
     for k in range(8):
         w_core_in(k).wait_recv()
 
-    def x_out(y, n, step, d):
-        terms, got = ((terms_a, got_a), (terms_b, got_b))[n]
-        xd = (x + d) % 4
-        return remote(
-            terms.at[y, :, xd], got.at[y, d - 1],
-            xs.at[n, step, d - 1], xr.at[n, step, d - 1], {"head": hi * 4 + xd},
-        )
+    def x_out(y, n, step, way, kind):
+        terms, got, relay = ((terms_a, got_a, relay_a), (terms_b, got_b, relay_b))[n]
+        xd = (x + 1 + 2 * way) % 4
+        if kind == 0:
+            src, dst = terms.at[y, way, :, (x + 2) % 4], relay.at[y, way]
+        else:
+            half = 1 - way if kind == 1 else way
+            src, dst = terms.at[y, half, :, xd], got.at[y, way, half]
+        sem = (n, step, way, kind)
+        return remote(src, dst, xs.at[sem], xr.at[sem], {"head": hi * 4 + xd})
 
     def project(y, n, step):
         first, width = WIDE[n]
@@ -310,9 +309,19 @@
         left = t[:, :width].reshape(16, 8, width)
         right = t[:, width:].reshape(16, 8, width)
         both = jnp.concatenate([left, right], axis=1).astype(BF16)
-        terms[y] = both.reshape(4, 4, 16, width)
-        for d in (2, 1, 3):
-            x_out(y, n, step, d).start()
+        terms[y] = both.reshape(2, 2, 4, 16, width)
+        for kind in range(2):
+            for way in range(2):
+                x_out(y, n, step, way, kind).start()
+
+    def pass_on(y, n, step):
+        terms, relay = ((terms_a, relay_a), (terms_b, relay_b))[n]
+        for way in range(2):
+            x_out(y, n, step, way, 0).wait_recv()
+            xd = (x + 1 + 2 * way) % 4
+            t = terms[y, way, :, xd].astype(F32) + relay[y, way].astype(F32)
+            terms[y, way, :, xd] = t.astype(BF16)
+            x_out(y, n, step, way, 2).start()
 
     def y_same(n, e):
         part, fin = ((part_a, fin_a), (part_b, fin_b))[n]
@@ -331,19 +340,23 @@
 
     def combine(y, n, step):
         terms, got, part = ((terms_a, got_a, part_a), (terms_b, got_b, part_b))[n]
-        for d in (1, 2, 3):
-            x_out(y, n, step, d).wait_recv()
-        t = terms[y, :, x].astype(F32)
-        for d in range(3):
-            t = t + got[y, d].astype(F32)
-        part[y] = t.astype(BF16)
-
-    for n in range(2):
-        project(lo, n, 0)
+        width = WIDE[n][1]
+        for way in range(2):
+            x_out(y, n, step, way, 1).wait_recv()
+            x_out(y, n, step, way, 2).wait_recv()
+        t = terms[y, :, :, x].astype(F32) + got[y, 0].astype(F32) + got[y, 1].astype(F32)
+        part[y] = t.reshape(4, 16, width).astype(BF16)
+
+    project(lo, 0, 0)
+    project(lo, 1, 0)
+    pass_on(lo, 0, 0)
     for i in range(4):
         v_in(i).wait_recv()
-    for n in range(2):
-        project(1 - lo, n, 1)
+    project(1 - lo, 0, 1)
+    pass_on(lo, 1, 0)
+    project(1 - lo, 1, 1)
+    pass_on(1 - lo, 0, 1)
+    pass_on(1 - lo, 1, 1)
     for n in range(2):
         combine(lo, n, 0)
         for e in (2, 1, 3):
@@ -384,10 +397,12 @@
     for k in range(8):
         w_core(k).wait_send()
     for n in range(2):
-        for d in (1, 2, 3):
-            x_out(lo, n, 0, d).wait_send()
-            x_out(1 - lo, n, 1, d).wait_send()
-            y_same(n, d).wait_send()
+        for way in range(2):
+            for kind in range(3):
+                x_out(lo, n, 0, way, kind).wait_send()
+                x_out(1 - lo, n, 1, way, kind).wait_send()
+        for e in (1, 2, 3):
+            y_same(n, e).wait_send()
         for e in range(4):
             y_other(n, e).wait_send()
 
@@ -398,12 +413,9 @@
     dma = pltpu.SemaphoreType.DMA
     rows = TOKENS * HEADS
     scratch = [
-        pltpu.VMEM((TOKENS, HEADS, NOPE + ROT), BF16),
-        pltpu.VMEM((rows, 128), F32),
-        pltpu.VMEM((rows, 128), F32),
+        pltpu.VMEM((HEADS, NOPE + ROT, TOKENS), BF16),
         pltpu.VMEM((HEADS, NOPE, LAT), BF16),
         pltpu.VMEM((HEADS, LAT, VAL), BF16),
-        pltpu.VMEM((rows, COLS), BF16),
         pltpu.VMEM((rows, WIDTH), BF16),
         pltpu.VMEM((TOKENS, SPAN * TOKENS), F32),
         pltpu.VMEM((16, 16, 384), BF16),
@@ -413,10 +425,12 @@
         pltpu.VMEM((rows, 128), F32),
         pltpu.VMEM((rows, 128), F32),
         pltpu.VMEM((rows, LAT), F32),
-        pltpu.VMEM((2, 4, 4, 16, 512), BF16),
-        pltpu.VMEM((2, 4, 4, 16, 384), BF16),
-        pltpu.VMEM((2, 3, 4, 16, 512), BF16),
-        pltpu.VMEM((2, 3, 4, 16, 384), BF16),
+        pltpu.VMEM((2, 2, 2, 4, 16, 512), BF16),
+        pltpu.VMEM((2, 2, 2, 4, 16, 384), BF16),
+        pltpu.VMEM((2, 2, 2, 2, 16, 512), BF16),
+        pltpu.VMEM((2, 2, 2, 2, 16, 384), BF16),
+        pltpu.VMEM((2, 2, 2, 16, 512), BF16),
+        pltpu.VMEM((2, 2, 2, 16, 384), BF16),
         pltpu.VMEM((2, 4, 16, 512), BF16),
         pltpu.VMEM((2, 4, 16, 384), BF16),
         pltpu.VMEM((2, 4, 16, 512), BF16),
@@ -431,7 +445,7 @@
         dma((4,)), dma((4,)),
         dma((8,)), dma((8,)),
         dma((4,)), dma((4,)),
-        dma((2, 2, 3)), dma((2, 2, 3)),
+        dma((2, 2, 2, 3)), dma((2, 2, 2, 3)),
         dma((2, 4)), dma((2, 4)),
         dma((2, 4)), dma((2, 4)),
     ]
@@ -442,10 +456,10 @@
         out_specs=vmem,
         scratch_shapes=scratch,
         compiler_params=pltpu.CompilerParams(
-            collective_id=0, has_side_effects=True, vmem_limit_bytes=48 * 1024 * 1024
+            collective_id=0, has_side_effects=True, vmem_limit_bytes=60 * 1024 * 1024
         ),
         cost_estimate=pl.CostEstimate(flops=3_500_000_000, bytes_accessed=3_000_000, transcendentals=1_048_576),
-    )(block_order, latent, queries, key_up_weight, value_up_weight, w_o)
+    )(block_order, latent, queries.transpose(1, 2, 0), key_up_weight, value_up_weight, w_o.T)
     return summed.reshape(2, 8, 8, 2 * COLS).transpose(1, 2, 0, 3).reshape(8, 32 * COLS).astype(BF16)
 
 

time: 74.1 us -> 71.9 us (0.970)
  local copies, waits for them, and re-layouts: 4.79 us -> 0.97 us
  other arithmetic: 0.01 us -> 0.91 us
  Pallas kernels: 69 us -> 69.8 us
    unnamed x10 -> x0, local copies, waits for them, and re-layouts: 3.83 us -> none
    convert_element_type x1, other arithmetic: 0.01 us -> 0.91 us  [shards(): summed.reshape(2, 8, 8, 2 * COLS).transpose(1, 2, 0, 3)]
    pallas_call x1, Pallas kernels: 69 us -> 69.8 us  [shards(): pl.pallas_call(kernel, out_shape=jax.ShapeDtypeStruct((2, 8, MINE), F32),...]
where the time goes in v2:
time: 71.9 us; the launch traced here: 71.7 us
  Pallas kernels  69.8 us (97%)
  local copies, waits for them, and re-layouts  0.97 us (1%)
  other arithmetic  0.91 us (1%)
    pallas_call x1, Pallas kernels, shards(): pl.pallas_call(kernel, out_shape=jax.ShapeDtypeStruct((2, 8, MINE), F32),...  69.8 us

profile of v2, /device:TPU:8, one launch (start us, length us, event | category | flops | bytes accessed | tf_op | source)
XLA Modules:
  0.0 71.7 jit_solution(13299614896006276742)
XLA Ops:
  0.0 69.8 %shard_map.64 = f32[2,8,1792]{2,1,0:T(8,128)} custom-call(s32[64]{0:T(128)} %order.1, bf16[8,576]{1,0:T(8,128)(2,1)} %latent.1, bf16[8,192,128]{2,1,0:T(8,128)(2,1)} %bitcast.4, bf16[8,128,512]{2,1,0:T(8,128)(2,1)} %ku_hbm.1, bf16[8,512,128]{2,1,0:T(8,128)(2,1)} %vu_hbm.1, bf16[112,1024]{1,0:T(8,128)(2,1)} %bitcast.5), custom_call_target="tpu_custom_call" | custom-call | flops 3500000000 | bytes 3000000 | tf_op jit(solution)/shard_map/pallas_call | solution.py:452
  69.8 0.9 %convert_element_type.12 = bf16[2,8,1792]{2,1,0:T(8,128)(2,1)S(1)} convert(f32[2,8,1792]{2,1,0:T(8,128)} %shard_map.64) | non-fusion elementwise | flops 28672 | bytes 172032 | tf_op jit(solution)/shard_map/convert_element_type | solution.py:463
  70.7 0.1 convert_element_type.13
  70.9 0.1 copy.7
  71.0 0.8 %convert_element_type.15 = bf16[8,3584]{1,0:T(8,128)(2,1)} reshape(bf16[8,8,2,224]{3,2,1,0:T(2,128)(2,1)S(1)} %copy.7) | data formatting | bytes 114688 | tf_op jit(solution)/shard_map/convert_element_type | solution.py:463

commit v3 on v2

--- a/solution.py
+++ b/solution.py
@@ -93,10 +93,6 @@
     def own_rows(i):
         return remote(pack.at[h], pack.at[h], ps.at[i], pr.at[i], {"head": (h + i) % 16})
 
-    @pl.loop(1, 16)
-    def _(i):
-        own_rows(i).start()
-
     def shard(zz, cc):
         return wt.at[pl.ds(pl.multiple_of((zz * 2 + cc) * COLS, 16), COLS)]
 
@@ -129,6 +125,11 @@
     loads[3].wait()
     w_plus(0).start()
     w_minus(0).start()
+
+    @pl.loop(1, 16)
+    def _(i):
+        own_rows(i).start()
+
     w_core(0).start()
 
     loads[0].wait()
@@ -153,6 +154,10 @@
         ref = pack.at[(h + 16 - i) % 16]
         remote(ref, ref, ps.at[i], pr.at[i], {"head": (h + i) % 16}).wait_recv()
 
+    def part_slot(plane, cc, half):
+        first = (8 - 4 * plane + cc) * TOKENS + half * HALF
+        return keys.at[pl.ds(pl.multiple_of(first, HALF), HALF)]
+
     def slot(plane, cc):
         return keys.at[pl.ds(pl.multiple_of((8 - 4 * plane + cc) * TOKENS, TOKENS), TOKENS)]
 
@@ -161,11 +166,13 @@
     keys[pl.ds(base, TOKENS), :384] = gathered[:, :8, :].reshape(TOKENS, 384).astype(BF16)
     keys[pl.ds(base, TOKENS), 384:] = gathered[:, 8:, :192].reshape(TOKENS, 192).astype(BF16)
 
-    def l_up(k):
-        return remote(slot(k, c), slot(k + 1, c), lzs.at[k], lzr.at[k], {"blk": up})
-
-    def l_up_in(k):
-        return remote(slot(k + 1, c), slot(k + 1, c), lzs.at[k], lzr.at[k], {"blk": up})
+    def l_up(k, half):
+        src, dst = part_slot(k, c, half), part_slot(k + 1, c, half)
+        return remote(src, dst, lzs.at[k, half], lzr.at[k, half], {"blk": up})
+
+    def l_up_in(k, half):
+        ref = part_slot(k + 1, c, half)
+        return remote(ref, ref, lzs.at[k, half], lzr.at[k, half], {"blk": up})
 
     def l_core(p):
         return remote(slot(p, c), slot(p, c), lcs.at[p], lcr.at[p], {"blk": mate})
@@ -173,13 +180,13 @@
     def l_core_in(p):
         return remote(slot(p, c_mate), slot(p, c_mate), lcs.at[p], lcr.at[p], {"blk": mate})
 
-    def l_side(j):
-        ref = slot(j + lo, c)
-        return remote(ref, ref, lys.at[j], lyr.at[j], {"blk": side})
-
-    def l_side_in(j):
-        ref = slot(j + 1 - lo, c_side)
-        return remote(ref, ref, lys.at[j], lyr.at[j], {"blk": side})
+    def l_side(j, half):
+        ref = part_slot(j + lo, c, half)
+        return remote(ref, ref, lys.at[j, half], lyr.at[j, half], {"blk": side})
+
+    def l_side_in(j, half):
+        ref = part_slot(j + 1 - lo, c_side, half)
+        return remote(ref, ref, lys.at[j, half], lyr.at[j, half], {"blk": side})
 
     def l_diag(j):
         ref = slot(j + 1 - lo, c_side)
@@ -201,30 +208,35 @@
             w_minus(k).start()
         w_core(3 + k).start()
 
-    l_up(0).start()
+    l_up(0, 0).start()
+    l_up(0, 1).start()
 
     @pl.when(lo == 0)
     def _():
-        l_side(0).start()
+        l_side(0, 0).start()
+        l_side(0, 1).start()
 
     l_core(0).start()
-
     w_step_minus(1)
-    l_up_in(0).wait_recv()
-    l_up(1).start()
-
-    @pl.when(lo == 0)
-    def _():
-        l_side(1).start()
-
-    @pl.when(lo == 1)
-    def _():
-        l_side(0).start()
+    for half in range(2):
+        l_up_in(0, half).wait_recv()
+        l_up(1, half).start()
+        l_side(1 - lo, half).start()
 
     l_core(1).start()
     w_step_plus(1)
-    l_side_in(0).wait_recv()
+    l_side_in(0, 0).wait_recv()
+    l_side_in(0, 1).wait_recv()
     l_diag(0).start()
+    for half in range(2):
+        l_up_in(1, half).wait_recv()
+
+        @pl.when(lo == 1)
+        def _():
+            l_side(1, half).start()
+
+    l_core(2).start()
+    w_step_minus(2)
     l_core_in(0).wait_recv()
     l_core_in(1).wait_recv()
     l_diag_in(0).wait_recv()
@@ -268,26 +280,19 @@
         v_out(i).start()
 
     pl.loop(0, 2)(near)
-    w_step_minus(2)
     w_step_plus(2)
-    l_up_in(1).wait_recv()
-
-    @pl.when(lo == 1)
-    def _():
-        l_side(1).start()
-
-    l_core(2).start()
+    l_side_in(1, 0).wait_recv()
+    l_side_in(1, 1).wait_recv()
+    l_diag(1).start()
     pl.loop(2, 4)(near)
-    l_side_in(1).wait_recv()
-    l_diag(1).start()
     w_step_minus(3)
-    w_step_plus(3)
     loads[2].wait()
     l_core_in(2).wait_recv()
     l_diag_in(1).wait_recv()
     pl.loop(0, 2)(far)
+    w_step_plus(3)
+    pl.loop(2, 4)(far)
     w_step_minus(4)
-    pl.loop(2, 4)(far)
     for k in range(8):
         w_core_in(k).wait_recv()
 
@@ -365,7 +370,8 @@
         combine(1 - lo, n, 1)
         for e in (2, 1, 3, 0):
             y_other(n, e).start()
-    for n, (first, width) in enumerate(WIDE):
+    same_cols, other_cols = [], []
+    for n in range(2):
         part, fin = ((part_a, fin_a), (part_b, fin_b))[n]
         same = part[lo, hi].astype(F32)
         for e in (1, 2, 3):
@@ -376,17 +382,24 @@
         for e in (1, 2, 3):
             y_other(n, e).wait_recv()
             other = other + fin[1, e].astype(F32)
-        for y, v in ((lo, same), (1 - lo, other)):
-            out[y, :, first:first + width] = v[:8]
-            out[y, :, first + width:first + 2 * width] = v[8:]
+        same_cols += [same[:8], same[8:]]
+        other_cols += [other[:8], other[8:]]
+    same = jnp.concatenate(same_cols, axis=1)
+    other = jnp.concatenate(other_cols, axis=1)
+    by_y = (jnp.where(lo == 0, same, other), jnp.where(lo == 0, other, same))
+    pair = 2 * COLS
+    out[...] = jnp.concatenate(
+        [by_y[i % 2][:, i // 2 * pair:(i // 2 + 1) * pair] for i in range(16)], axis=1
+    ).astype(BF16)
 
     @pl.loop(1, 16)
     def _(i):
         own_rows(i).wait_send()
 
     for k in range(2):
-        l_up(k).wait_send()
-        l_side(k).wait_send()
+        for half in range(2):
+            l_up(k, half).wait_send()
+            l_side(k, half).wait_send()
         l_diag(k).wait_send()
     for k in range(3):
         l_core(k).wait_send()
@@ -437,9 +450,9 @@
         pltpu.VMEM((2, 4, 16, 384), BF16),
         dma((4,)),
         dma((16,)), dma((16,)),
-        dma((2,)), dma((2,)),
+        dma((2, 2)), dma((2, 2)),
         dma((3,)), dma((3,)),
-        dma((2,)), dma((2,)),
+        dma((2, 2)), dma((2, 2)),
         dma((2,)), dma((2,)),
         dma((3,)), dma((3,)),
         dma((4,)), dma((4,)),
@@ -449,9 +462,9 @@
         dma((2, 4)), dma((2, 4)),
         dma((2, 4)), dma((2, 4)),
     ]
-    summed = pl.pallas_call(
+    return pl.pallas_call(
         kernel,
-        out_shape=jax.ShapeDtypeStruct((2, 8, MINE), F32),
+        out_shape=jax.ShapeDtypeStruct((8, 2 * MINE), BF16),
         in_specs=[pl.BlockSpec(memory_space=pltpu.SMEM), vmem] + [anywhere] * 4,
         out_specs=vmem,
         scratch_shapes=scratch,
@@ -460,7 +473,6 @@
         ),
         cost_estimate=pl.CostEstimate(flops=3_500_000_000, bytes_accessed=3_000_000, transcendentals=1_048_576),
     )(block_order, latent, queries.transpose(1, 2, 0), key_up_weight, value_up_weight, w_o.T)
-    return summed.reshape(2, 8, 8, 2 * COLS).transpose(1, 2, 0, 3).reshape(8, 32 * COLS).astype(BF16)
 
 
 def solution(mesh):

time: 71.9 us -> 68.6 us (0.954)
  the two profiles are of different devices: /device:TPU:8 before, /device:TPU:1 now
where the time goes in v3:
time: 68.6 us; the launch traced here: 68.4 us
  Pallas kernels  66.9 us (98%)
  local copies, waits for them, and re-layouts  1.45 us (2%)
    pallas_call x1, Pallas kernels, shards(): pl.pallas_call(kernel, out_shape=jax.ShapeDtypeStruct((8, 2 * MINE), BF16...  66.9 us
    unnamed x1, local copies, waits for them, and re-layouts  1.45 us

profile of v3, /device:TPU:1, one launch (start us, length us, event | category | flops | bytes accessed | tf_op | source)
XLA Modules:
  0.0 68.4 jit_solution(16355742796539981043)
XLA Ops:
  0.0 66.9 %shard_map.64 = bf16[8,3584]{1,0:T(8,128)(2,1)} custom-call(s32[64]{0:T(128)} %order.1, bf16[8,576]{1,0:T(8,128)(2,1)} %latent.1, bf16[8,192,128]{2,1,0:T(8,128)(2,1)} %bitcast.2, bf16[8,128,512]{2,1,0:T(8,128)(2,1)} %ku_hbm.1, bf16[8,512,128]{2,1,0:T(8,128)(2,1)} %vu_hbm.1, bf16[112,1024]{1,0:T(8,128)(2,1)} %bitcast.3), custom_call_target="tpu_custom_call" | custom-call | flops 3500000000 | bytes 3000000 | tf_op jit(solution)/shard_map/pallas_call | solution.py:465
  66.9 1.4 %copy.8 = bf16[8,3584]{1,0:T(8,128)(2,1)} copy(bf16[8,3584]{1,0:T(8,128)(2,1)} %shard_map.64) | data formatting | bytes 114688

commit v4 on v3

--- a/solution.py
+++ b/solution.py
@@ -42,7 +42,7 @@
 def kernel(
     order, latent, q_hbm, ku_hbm, vu_hbm, wo_hbm, out,
     q_raw, ku, vu, q_full, bias, pack, keys, wt, vals,
-    top, total, accum, terms_a, terms_b, got_a, got_b, relay_a, relay_b, part_a, part_b, fin_a, fin_b,
+    top, total, accum, score, prob, ctx, terms_a, terms_b, got_a, got_b, relay_a, relay_b, part_a, part_b, fin_a, fin_b,
     load_sem, ps, pr, lzs, lzr, lcs, lcr, lys, lyr, lds, ldr,
     wps, wpr, wms, wmr, wcs, wcr, vs, vr, xs, xr, yss, ysr, yos, yor,
 ):
@@ -135,11 +135,14 @@
     loads[0].wait()
     loads[1].wait()
     for n in range(HEADS):
-        at = slice(n * TOKENS, (n + 1) * TOKENS)
-        q_full[at, :LAT] = lax.dot_general(
+        lat = lax.dot_general(
             q_raw[n, :NOPE, :], ku[n], (((0,), (0,)), ((), ())), preferred_element_type=F32
         ).astype(BF16)
-        q_full[at, LAT:] = q_raw[n, NOPE:, :].astype(F32).T.astype(BF16)
+        turned = q_raw[n, NOPE:, :].astype(F32).T.astype(BF16)
+        for t in range(2):
+            at = slice(t * 512 + n * HALF, t * 512 + (n + 1) * HALF)
+            q_full[at, :LAT] = lat[t * HALF:(t + 1) * HALF]
+            q_full[at, LAT:] = turned[t * HALF:(t + 1) * HALF]
 
     row = lax.broadcasted_iota(jnp.int32, (TOKENS, TOKENS), 0)
     col = lax.broadcasted_iota(jnp.int32, (TOKENS, TOKENS), 1)
@@ -241,147 +244,172 @@
     l_core_in(1).wait_recv()
     l_diag_in(0).wait_recv()
 
-    def scores(i, start, first):
-        q = q_full[pl.ds(pl.multiple_of(i * 256, 256), 256), :]
+    def v_out(t):
+        ref = vals.at[t, lo]
+        return remote(ref, ref, vs.at[t], vr.at[t], {"blk": side})
+
+    def v_in(t):
+        ref = vals.at[t, 1 - lo]
+        return remote(ref, ref, vs.at[t], vr.at[t], {"blk": side})
+
+    def rows_at(t, g, first, count):
+        return pl.ds(pl.multiple_of(t * 512 + g * 256 + first, 32), count)
+
+    def step(t, start, first, last):
         k = keys[pl.ds(pl.multiple_of(start, TOKENS), 512), :]
-        sc = nt_dot(q, k).reshape(2, TOKENS, 512) + bias[:, first:first + 512][None]
-        return sc.reshape(256, 512), k
-
-    def near(i):
-        at = pl.ds(pl.multiple_of(i * 256, 256), 256)
-        sc, k = scores(i, (c + 5) * TOKENS, 512)
-        m = jnp.max(sc, axis=1, keepdims=True)
-        e = jnp.exp2((sc - m) * GAIN)
-        top[at, :] = jnp.broadcast_to(m, (256, 128))
-        total[at, :] = jnp.broadcast_to(jnp.sum(e, axis=1, keepdims=True), (256, 128))
-        accum[at, :] = jnp.dot(e.astype(BF16), k[:, :LAT], preferred_element_type=F32)
-
-    def v_out(i):
-        ref = vals.at[lo, :, pl.ds(pl.multiple_of(i * 256, 256), 256)]
-        return remote(ref, ref, vs.at[i], vr.at[i], {"blk": side})
-
-    def v_in(i):
-        ref = vals.at[1 - lo, :, pl.ds(pl.multiple_of(i * 256, 256), 256)]
-        return remote(ref, ref, vs.at[i], vr.at[i], {"blk": side})
-
-    def far(i):
-        at = pl.ds(pl.multiple_of(i * 256, 256), 256)
-        sc, k = scores(i, (c + 1) * TOKENS, 0)
-        old = top[at, :][:, :1]
-        m = jnp.maximum(old, jnp.max(sc, axis=1, keepdims=True))
-        e = jnp.exp2((sc - m) * GAIN)
-        shrink = jnp.exp2((old - m) * GAIN)
-        tot = total[at, :][:, :1] * shrink + jnp.sum(e, axis=1, keepdims=True)
-        acc = accum[at, :] * shrink + jnp.dot(e.astype(BF16), k[:, :LAT], preferred_element_type=F32)
-        ctx = (acc * (1.0 / tot)).astype(BF16)
-        for n in range(2):
-            v = jnp.dot(ctx[n * TOKENS:(n + 1) * TOKENS], vu[2 * i + n], preferred_element_type=F32)
-            vals[lo, :, pl.ds(pl.multiple_of(i * 256 + n * VAL, VAL), VAL)] = v.astype(BF16)
-        v_out(i).start()
-
-    pl.loop(0, 2)(near)
-    w_step_plus(2)
-    l_side_in(1, 0).wait_recv()
-    l_side_in(1, 1).wait_recv()
-    l_diag(1).start()
-    pl.loop(2, 4)(near)
+        for g in range(2):
+            score[g] = nt_dot(q_full[rows_at(t, g, 0, 256), :], k)
+        for g in range(2):
+            factors = []
+            for r in range(8):
+                at = rows_at(t, g, r * 32, 32)
+                tok = pl.ds(pl.multiple_of(t * HALF + r % 2 * 32, 32), 32)
+                sc = score[g, r * 32:(r + 1) * 32, :] + bias[tok, first:first + 512]
+                m = jnp.max(sc, axis=1, keepdims=True)
+                if last:
+                    old = top[at, :][:, :1]
+                    m = jnp.maximum(m, old)
+                e = jnp.exp2((sc - m) * GAIN)
+                add = jnp.sum(e, axis=1, keepdims=True)
+                prob[g, r * 32:(r + 1) * 32, :] = e.astype(BF16)
+                if last:
+                    shrink = jnp.exp2((old - m) * GAIN)
+                    inverse = 1.0 / (total[at, :][:, :1] * shrink + add)
+                    factors.append((shrink * inverse, inverse))
+                else:
+                    top[at, :] = jnp.broadcast_to(m, (32, 128))
+                    total[at, :] = jnp.broadcast_to(add, (32, 128))
+            got = jnp.dot(prob[g], k[:, :LAT], preferred_element_type=F32)
+            if not last:
+                accum[rows_at(t, g, 0, 256), :] = got
+                continue
+            score[g] = got
+            for r in range(8):
+                old, new = factors[r]
+                ctx[g, r * 32:(r + 1) * 32, :] = (
+                    accum[rows_at(t, g, r * 32, 32), :] * old + score[g, r * 32:(r + 1) * 32, :] * new
+                ).astype(BF16)
+            for n in range(4):
+                head = 4 * g + n
+                v = jnp.dot(ctx[g, n * HALF:(n + 1) * HALF, :], vu[head], preferred_element_type=F32)
+                vals[t, lo, :, head * VAL:(head + 1) * VAL] = v.astype(BF16)
+
+    @pl.loop(0, 2)
+    def _(t):
+        step(t, (c + 5) * TOKENS, 512, False)
+
+        @pl.when(t == 0)
+        def _():
+            w_step_plus(2)
+            l_side_in(1, 0).wait_recv()
+            l_side_in(1, 1).wait_recv()
+            l_diag(1).start()
+
     w_step_minus(3)
     loads[2].wait()
     l_core_in(2).wait_recv()
     l_diag_in(1).wait_recv()
-    pl.loop(0, 2)(far)
-    w_step_plus(3)
-    pl.loop(2, 4)(far)
+
+    @pl.loop(0, 2)
+    def _(t):
+        step(t, (c + 1) * TOKENS, 0, True)
+        v_out(t).start()
+
+        @pl.when(t == 0)
+        def _():
+            w_step_plus(3)
+
     w_step_minus(4)
     for k in range(8):
         w_core_in(k).wait_recv()
 
-    def x_out(y, n, step, way, kind):
+    def x_out(t, n, way, kind):
         terms, got, relay = ((terms_a, got_a, relay_a), (terms_b, got_b, relay_b))[n]
         xd = (x + 1 + 2 * way) % 4
         if kind == 0:
-            src, dst = terms.at[y, way, :, (x + 2) % 4], relay.at[y, way]
+            src, dst = terms.at[t, way, (x + 2) % 4], relay.at[t, way]
         else:
-            half = 1 - way if kind == 1 else way
-            src, dst = terms.at[y, half, :, xd], got.at[y, way, half]
-        sem = (n, step, way, kind)
+            r = 1 - way if kind == 1 else way
+            src, dst = terms.at[t, r, xd], got.at[t, way, r]
+        sem = (t, n, way, kind)
         return remote(src, dst, xs.at[sem], xr.at[sem], {"head": hi * 4 + xd})
 
-    def project(y, n, step):
+    def project(t, n):
         first, width = WIDE[n]
         terms = (terms_a, terms_b)[n]
-        t = nt_dot(vals[y], wt[first:first + 2 * width, :])
-        left = t[:, :width].reshape(16, 8, width)
-        right = t[:, width:].reshape(16, 8, width)
-        both = jnp.concatenate([left, right], axis=1).astype(BF16)
-        terms[y] = both.reshape(2, 2, 4, 16, width)
+        both = vals[t].reshape(TOKENS, HEADS * VAL)
+        out = nt_dot(both, wt[first:first + 2 * width, :])
+        for y in range(2):
+            left = out[y * HALF:(y + 1) * HALF, :width].reshape(8, 8, width)
+            right = out[y * HALF:(y + 1) * HALF, width:].reshape(8, 8, width)
+            pair = jnp.concatenate([left, right], axis=1).astype(BF16)
+            terms[t, :, :, y] = pair.reshape(2, 4, 16, width)
         for kind in range(2):
             for way in range(2):
-                x_out(y, n, step, way, kind).start()
-
-    def pass_on(y, n, step):
+                x_out(t, n, way, kind).start()
+
+    def pass_on(t, n):
         terms, relay = ((terms_a, relay_a), (terms_b, relay_b))[n]
         for way in range(2):
-            x_out(y, n, step, way, 0).wait_recv()
+            x_out(t, n, way, 0).wait_recv()
             xd = (x + 1 + 2 * way) % 4
-            t = terms[y, way, :, xd].astype(F32) + relay[y, way].astype(F32)
-            terms[y, way, :, xd] = t.astype(BF16)
-            x_out(y, n, step, way, 2).start()
-
-    def y_same(n, e):
+            both = terms[t, way, xd].astype(F32) + relay[t, way].astype(F32)
+            terms[t, way, xd] = both.astype(BF16)
+            x_out(t, n, way, 2).start()
+
+    def y_same(n, yd, src):
         part, fin = ((part_a, fin_a), (part_b, fin_b))[n]
-        yd = (hi + e) % 4
         return remote(
-            part.at[lo, yd], fin.at[0, e], yss.at[n, e], ysr.at[n, e], {"head": yd * 4 + x}
+            part.at[yd, lo], fin.at[0, src], yss.at[n, yd], ysr.at[n, src], {"head": yd * 4 + x}
         )
 
-    def y_other(n, e):
+    def y_other(n, yd, src):
         part, fin = ((part_a, fin_a), (part_b, fin_b))[n]
-        yd = (hi + e) % 4
         return remote(
-            part.at[1 - lo, yd], fin.at[1, e], yos.at[n, e], yor.at[n, e],
+            part.at[yd, 1 - lo], fin.at[1, src], yos.at[n, yd], yor.at[n, src],
             {"blk": side, "head": yd * 4 + x},
         )
 
-    def combine(y, n, step):
+    def combine(t, n):
         terms, got, part = ((terms_a, got_a, part_a), (terms_b, got_b, part_b))[n]
-        width = WIDE[n][1]
         for way in range(2):
-            x_out(y, n, step, way, 1).wait_recv()
-            x_out(y, n, step, way, 2).wait_recv()
-        t = terms[y, :, :, x].astype(F32) + got[y, 0].astype(F32) + got[y, 1].astype(F32)
-        part[y] = t.reshape(4, 16, width).astype(BF16)
-
-    project(lo, 0, 0)
-    project(lo, 1, 0)
-    pass_on(lo, 0, 0)
-    for i in range(4):
-        v_in(i).wait_recv()
-    project(1 - lo, 0, 1)
-    pass_on(lo, 1, 0)
-    project(1 - lo, 1, 1)
-    pass_on(1 - lo, 0, 1)
-    pass_on(1 - lo, 1, 1)
-    for n in range(2):
-        combine(lo, n, 0)
-        for e in (2, 1, 3):
-            y_same(n, e).start()
-    for n in range(2):
-        combine(1 - lo, n, 1)
-        for e in (2, 1, 3, 0):
-            y_other(n, e).start()
+            x_out(t, n, way, 1).wait_recv()
+            x_out(t, n, way, 2).wait_recv()
+        both = terms[t, :, x].astype(F32) + got[t, 0].astype(F32) + got[t, 1].astype(F32)
+        part[2 * t:2 * t + 2] = both.astype(BF16)
+        for yd in (2 * t, 2 * t + 1):
+            y_other(n, yd, hi).start()
+
+            @pl.when(hi != yd)
+            def _():
+                y_same(n, yd, hi).start()
+
+    v_in(0).wait_recv()
+    project(0, 0)
+    project(0, 1)
+    pass_on(0, 0)
+    v_in(1).wait_recv()
+    project(1, 0)
+    pass_on(0, 1)
+    project(1, 1)
+    combine(0, 0)
+    pass_on(1, 0)
+    combine(0, 1)
+    pass_on(1, 1)
+    combine(1, 0)
+    combine(1, 1)
     same_cols, other_cols = [], []
     for n in range(2):
         part, fin = ((part_a, fin_a), (part_b, fin_b))[n]
-        same = part[lo, hi].astype(F32)
+        same = part[hi, lo].astype(F32)
+        other = jnp.zeros_like(same)
         for e in (1, 2, 3):
-            y_same(n, e).wait_recv()
-            same = same + fin[0, e].astype(F32)
-        y_other(n, 0).wait_recv()
-        other = fin[1, 0].astype(F32)
-        for e in (1, 2, 3):
-            y_other(n, e).wait_recv()
-            other = other + fin[1, e].astype(F32)
+            src = (hi + e) % 4
+            y_same(n, src, src).wait_recv()
+            same = same + fin[0, src].astype(F32)
+        for src in range(4):
+            y_other(n, src, src).wait_recv()
+            other = other + fin[1, src].astype(F32)
         same_cols += [same[:8], same[8:]]
         other_cols += [other[:8], other[8:]]
     same = jnp.concatenate(same_cols, axis=1)
@@ -406,18 +434,19 @@
         w_plus(k).wait_send()
     for k in range(4):
         w_minus(k).wait_send()
-        v_out(k).wait_send()
     for k in range(8):
         w_core(k).wait_send()
+    for t in range(2):
+        v_out(t).wait_send()
     for n in range(2):
-        for way in range(2):
-            for kind in range(3):
-                x_out(lo, n, 0, way, kind).wait_send()
-                x_out(1 - lo, n, 1, way, kind).wait_send()
+        for t in range(2):
+            for way in range(2):
+                for kind in range(3):
+                    x_out(t, n, way, kind).wait_send()
+        for yd in range(4):
+            y_other(n, yd, hi).wait_send()
         for e in (1, 2, 3):
-            y_same(n, e).wait_send()
-        for e in range(4):
-            y_other(n, e).wait_send()
+            y_same(n, (hi + e) % 4, hi).wait_send()
 
 
 def shards(queries, latent, key_up_weight, value_up_weight, w_o, block_order):
@@ -434,18 +463,21 @@
         pltpu.VMEM((16, 16, 384), BF16),
         pltpu.VMEM((12 * TOKENS, WIDTH), BF16),
         pltpu.VMEM((MINE, HEADS * VAL), BF16),
-        pltpu.VMEM((2, TOKENS, HEADS * VAL), BF16),
+        pltpu.VMEM((2, 2, HALF, HEADS * VAL), BF16),
         pltpu.VMEM((rows, 128), F32),
         pltpu.VMEM((rows, 128), F32),
         pltpu.VMEM((rows, LAT), F32),
-        pltpu.VMEM((2, 2, 2, 4, 16, 512), BF16),
-        pltpu.VMEM((2, 2, 2, 4, 16, 384), BF16),
+        pltpu.VMEM((2, 256, LAT), F32),
+        pltpu.VMEM((2, 256, LAT), BF16),
+        pltpu.VMEM((2, 256, LAT), BF16),
+        pltpu.VMEM((2, 2, 4, 2, 16, 512), BF16),
+        pltpu.VMEM((2, 2, 4, 2, 16, 384), BF16),
         pltpu.VMEM((2, 2, 2, 2, 16, 512), BF16),
         pltpu.VMEM((2, 2, 2, 2, 16, 384), BF16),
         pltpu.VMEM((2, 2, 2, 16, 512), BF16),
         pltpu.VMEM((2, 2, 2, 16, 384), BF16),
-        pltpu.VMEM((2, 4, 16, 512), BF16),
-        pltpu.VMEM((2, 4, 16, 384), BF16),
+        pltpu.VMEM((4, 2, 16, 512), BF16),
+        pltpu.VMEM((4, 2, 16, 384), BF16),
         pltpu.VMEM((2, 4, 16, 512), BF16),
         pltpu.VMEM((2, 4, 16, 384), BF16),
         dma((4,)),
@@ -457,7 +489,7 @@
         dma((3,)), dma((3,)),
         dma((4,)), dma((4,)),
         dma((8,)), dma((8,)),
-        dma((4,)), dma((4,)),
+        dma((2,)), dma((2,)),
         dma((2, 2, 2, 3)), dma((2, 2, 2, 3)),
         dma((2, 4)), dma((2, 4)),
         dma((2, 4)), dma((2, 4)),

time: 68.6 us -> 67.5 us (0.984)
  the two profiles are of different devices: /device:TPU:1 before, /device:TPU:56 now
where the time goes in v4:
time: 67.5 us; the launch traced here: 67.3 us
  Pallas kernels  65.9 us (98%)
  local copies, waits for them, and re-layouts  1.45 us (2%)
    pallas_call x1, Pallas kernels, shards(): pl.pallas_call(kernel, out_shape=jax.ShapeDtypeStruct((8, 2 * MINE), BF16...  65.9 us
    unnamed x1, local copies, waits for them, and re-layouts  1.45 us

profile of v4, /device:TPU:56, one launch (start us, length us, event | category | flops | bytes accessed | tf_op | source)
XLA Modules:
  0.0 67.3 jit_solution(18119906653345224211)
XLA Ops:
  0.0 65.9 %shard_map.64 = bf16[8,3584]{1,0:T(8,128)(2,1)} custom-call(s32[64]{0:T(128)} %order.1, bf16[8,576]{1,0:T(8,128)(2,1)} %latent.1, bf16[8,192,128]{2,1,0:T(8,128)(2,1)} %bitcast.2, bf16[8,128,512]{2,1,0:T(8,128)(2,1)} %ku_hbm.1, bf16[8,512,128]{2,1,0:T(8,128)(2,1)} %vu_hbm.1, bf16[112,1024]{1,0:T(8,128)(2,1)} %bitcast.3), custom_call_target="tpu_custom_call" | custom-call | flops 3500000000 | bytes 3000000 | tf_op jit(solution)/shard_map/pallas_call | solution.py:497
  65.9 1.4 %copy.8 = bf16[8,3584]{1,0:T(8,128)(2,1)} copy(bf16[8,3584]{1,0:T(8,128)(2,1)} %shard_map.64) | data formatting | bytes 114688

commit v5 on v4

--- a/solution.py
+++ b/solution.py
@@ -93,44 +93,59 @@
     def own_rows(i):
         return remote(pack.at[h], pack.at[h], ps.at[i], pr.at[i], {"head": (h + i) % 16})
 
-    def shard(zz, cc):
-        return wt.at[pl.ds(pl.multiple_of((zz * 2 + cc) * COLS, 16), COLS)]
-
-    def w_plus(k):
-        ref = shard((z + 8 - k) % 8, core)
-        return remote(ref, ref, wps.at[k], wpr.at[k], {"blk": up})
-
-    def w_minus(k):
-        ref = shard((z + k) % 8, core)
-        return remote(ref, ref, wms.at[k], wmr.at[k], {"blk": down})
-
-    def w_core(k):
+    def shard(zz, cc, half):
+        first = (zz * 2 + cc) * COLS + 64 * half
+        return wt.at[pl.ds(pl.multiple_of(first, 16), (64, 48)[half])]
+
+    def w_plus(k, half):
+        ref = shard((z + 8 - k) % 8, core, half)
+        return remote(ref, ref, wps.at[k, half], wpr.at[k, half], {"blk": up})
+
+    def w_minus(k, half):
+        ref = shard((z + k) % 8, core, half)
+        return remote(ref, ref, wms.at[k, half], wmr.at[k, half], {"blk": down})
+
+    def w_core(k, half):
         zz = (z + 8 - k) % 8 if k < 4 else (z + k - 3) % 8
-        ref = shard(zz, core)
-        return remote(ref, ref, wcs.at[k], wcr.at[k], {"blk": mate})
-
-    def w_core_in(k):
+        ref = shard(zz, core, half)
+        return remote(ref, ref, wcs.at[k, half], wcr.at[k, half], {"blk": mate})
+
+    def w_core_in(k, half):
         zz = (z + 8 - k) % 8 if k < 4 else (z + k - 3) % 8
-        ref = shard(zz, 1 - core)
-        return remote(ref, ref, wcs.at[k], wcr.at[k], {"blk": mate})
-
-    def w_plus_in(k):
-        ref = shard((z + 7 - k) % 8, core)
-        return remote(ref, ref, wps.at[k], wpr.at[k], {"blk": up})
-
-    def w_minus_in(k):
-        ref = shard((z + 1 + k) % 8, core)
-        return remote(ref, ref, wms.at[k], wmr.at[k], {"blk": down})
+        ref = shard(zz, 1 - core, half)
+        return remote(ref, ref, wcs.at[k, half], wcr.at[k, half], {"blk": mate})
+
+    def w_plus_in(k, half):
+        ref = shard((z + 7 - k) % 8, core, half)
+        return remote(ref, ref, wps.at[k, half], wpr.at[k, half], {"blk": up})
+
+    def w_minus_in(k, half):
+        ref = shard((z + 1 + k) % 8, core, half)
+        return remote(ref, ref, wms.at[k, half], wmr.at[k, half], {"blk": down})
+
+    def w_step_plus(k, half):
+        w_plus_in(k - 1, half).wait_recv()
+        if k < 3:
+            w_plus(k, half).start()
+        w_core(k, half).start()
+
+    def w_step_minus(k, half):
+        w_minus_in(k - 1, half).wait_recv()
+        if k < 4:
+            w_minus(k, half).start()
+        w_core(3 + k, half).start()
 
     loads[3].wait()
-    w_plus(0).start()
-    w_minus(0).start()
+    for half in range(2):
+        w_plus(0, half).start()
+        w_minus(0, half).start()
 
     @pl.loop(1, 16)
     def _(i):
         own_rows(i).start()
 
-    w_core(0).start()
+    for half in range(2):
+        w_core(0, half).start()
 
     loads[0].wait()
     loads[1].wait()
@@ -199,18 +214,6 @@
         ref = slot(j + 1 - lo, c_diag)
         return remote(ref, ref, lds.at[j], ldr.at[j], {"blk": mate})
 
-    def w_step_plus(k):
-        w_plus_in(k - 1).wait_recv()
-        if k < 3:
-            w_plus(k).start()
-        w_core(k).start()
-
-    def w_step_minus(k):
-        w_minus_in(k - 1).wait_recv()
-        if k < 4:
-            w_minus(k).start()
-        w_core(3 + k).start()
-
     l_up(0, 0).start()
     l_up(0, 1).start()
 
@@ -220,14 +223,18 @@
         l_side(0, 1).start()
 
     l_core(0).start()
-    w_step_minus(1)
+    for half in range(2):
+        w_step_minus(1, half)
+        w_step_plus(1, half)
     for half in range(2):
         l_up_in(0, half).wait_recv()
         l_up(1, half).start()
         l_side(1 - lo, half).start()
 
     l_core(1).start()
-    w_step_plus(1)
+    for half in range(2):
+        w_step_minus(2, half)
+        w_step_plus(2, half)
     l_side_in(0, 0).wait_recv()
     l_side_in(0, 1).wait_recv()
     l_diag(0).start()
@@ -239,7 +246,8 @@
             l_side(1, half).start()
 
     l_core(2).start()
-    w_step_minus(2)
+    for half in range(2):
+        w_step_minus(3, half)
     l_core_in(0).wait_recv()
     l_core_in(1).wait_recv()
     l_diag_in(0).wait_recv()
@@ -300,12 +308,12 @@
 
         @pl.when(t == 0)
         def _():
-            w_step_plus(2)
             l_side_in(1, 0).wait_recv()
             l_side_in(1, 1).wait_recv()
             l_diag(1).start()
 
-    w_step_minus(3)
+    for half in range(2):
+        w_step_plus(3, half)
     loads[2].wait()
     l_core_in(2).wait_recv()
     l_diag_in(1).wait_recv()
@@ -317,11 +325,12 @@
 
         @pl.when(t == 0)
         def _():
-            w_step_plus(3)
-
-    w_step_minus(4)
+            for half in range(2):
+                w_step_minus(4, half)
+
     for k in range(8):
-        w_core_in(k).wait_recv()
+        for half in range(2):
+            w_core_in(k, half).wait_recv()
 
     def x_out(t, n, way, kind):
         terms, got, relay = ((terms_a, got_a, relay_a), (terms_b, got_b, relay_b))[n]
@@ -431,11 +440,13 @@
         l_diag(k).wait_send()
     for k in range(3):
         l_core(k).wait_send()
-        w_plus(k).wait_send()
-    for k in range(4):
-        w_minus(k).wait_send()
-    for k in range(8):
-        w_core(k).wait_send()
+    for half in range(2):
+        for k in range(3):
+            w_plus(k, half).wait_send()
+        for k in range(4):
+            w_minus(k, half).wait_send()
+        for k in range(8):
+            w_core(k, half).wait_send()
     for t in range(2):
         v_out(t).wait_send()
     for n in range(2):
@@ -486,9 +497,9 @@
         dma((3,)), dma((3,)),
         dma((2, 2)), dma((2, 2)),
         dma((2,)), dma((2,)),
-        dma((3,)), dma((3,)),
-        dma((4,)), dma((4,)),
-        dma((8,)), dma((8,)),
+        dma((3, 2)), dma((3, 2)),
+        dma((4, 2)), dma((4, 2)),
+        dma((8, 2)), dma((8, 2)),
         dma((2,)), dma((2,)),
         dma((2, 2, 2, 3)), dma((2, 2, 2, 3)),
         dma((2, 4)), dma((2, 4)),

time: 67.5 us -> 70.3 us (1.041)
  Pallas kernels: 65.9 us -> 68.6 us
    pallas_call x1, Pallas kernels: 65.9 us -> 68.6 us  [shards(): pl.pallas_call(kernel, out_shape=jax.ShapeDtypeStruct((8, 2 * MINE), BF16...]
where the time goes in v5:
time: 70.3 us; the launch traced here: 70.1 us
  Pallas kernels  68.6 us (98%)
  local copies, waits for them, and re-layouts  1.45 us (2%)
    pallas_call x1, Pallas kernels, shards(): pl.pallas_call(kernel, out_shape=jax.ShapeDtypeStruct((8, 2 * MINE), BF16...  68.6 us
    unnamed x1, local copies, waits for them, and re-layouts  1.45 us

profile of v5, /device:TPU:56, one launch (start us, length us, event | category | flops | bytes accessed | tf_op | source)
XLA Modules:
  0.0 70.1 jit_solution(4251139508398537968)
XLA Ops:
  0.0 68.6 %shard_map.64 = bf16[8,3584]{1,0:T(8,128)(2,1)} custom-call(s32[64]{0:T(128)} %order.1, bf16[8,576]{1,0:T(8,128)(2,1)} %latent.1, bf16[8,192,128]{2,1,0:T(8,128)(2,1)} %bitcast.2, bf16[8,128,512]{2,1,0:T(8,128)(2,1)} %ku_hbm.1, bf16[8,512,128]{2,1,0:T(8,128)(2,1)} %vu_hbm.1, bf16[112,1024]{1,0:T(8,128)(2,1)} %bitcast.3), custom_call_target="tpu_custom_call" | custom-call | flops 3500000000 | bytes 3000000 | tf_op jit(solution)/shard_map/pallas_call | solution.py:508
  68.6 1.4 %copy.8 = bf16[8,3584]{1,0:T(8,128)(2,1)} copy(bf16[8,3584]{1,0:T(8,128)(2,1)} %shard_map.64) | data formatting | bytes 114688

commit v6 on v3

--- a/solution.py
+++ b/solution.py
@@ -23,13 +23,8 @@
 WIDE = ((0, 512), (1024, 384))
 GAIN = (NOPE + ROT) ** (-0.5) * math.log2(math.e)
 HIDDEN = -1e30
-NT = (((1,), (1,)), ((), ()))
 F32 = jnp.float32
 BF16 = jnp.bfloat16
-
-
-def nt_dot(a, b):
-    return lax.dot_general(a, b, NT, preferred_element_type=F32)
 
 
 def remote(src, dst, send, recv, device):
@@ -41,8 +36,8 @@
 
 def kernel(
     order, latent, q_hbm, ku_hbm, vu_hbm, wo_hbm, out,
-    q_raw, ku, vu, q_full, bias, pack, keys, wt, vals,
-    top, total, accum, terms_a, terms_b, got_a, got_b, relay_a, relay_b, part_a, part_b, fin_a, fin_b,
+    q_raw, ku, vu, vu_t, q_t, bias, pack, keys, near_keys, keys_t, wt, vals,
+    top, total, accum, score, prob, terms_a, terms_b, got_a, got_b, relay_a, relay_b, part_a, part_b, fin_a, fin_b,
     load_sem, ps, pr, lzs, lzr, lcs, lcr, lys, lyr, lds, ldr,
     wps, wpr, wms, wmr, wcs, wcr, vs, vr, xs, xr, yss, ysr, yos, yor,
 ):
@@ -93,61 +88,85 @@
     def own_rows(i):
         return remote(pack.at[h], pack.at[h], ps.at[i], pr.at[i], {"head": (h + i) % 16})
 
-    def shard(zz, cc):
-        return wt.at[pl.ds(pl.multiple_of((zz * 2 + cc) * COLS, 16), COLS)]
-
-    def w_plus(k):
-        ref = shard((z + 8 - k) % 8, core)
-        return remote(ref, ref, wps.at[k], wpr.at[k], {"blk": up})
-
-    def w_minus(k):
-        ref = shard((z + k) % 8, core)
-        return remote(ref, ref, wms.at[k], wmr.at[k], {"blk": down})
-
-    def w_core(k):
+    def shard(zz, cc, half):
+        first = (zz * 2 + cc) * COLS + 64 * half
+        return wt.at[pl.ds(pl.multiple_of(first, 16), (64, 48)[half])]
+
+    def w_plus(k, half):
+        ref = shard((z + 8 - k) % 8, core, half)
+        return remote(ref, ref, wps.at[k, half], wpr.at[k, half], {"blk": up})
+
+    def w_minus(k, half):
+        ref = shard((z + k) % 8, core, half)
+        return remote(ref, ref, wms.at[k, half], wmr.at[k, half], {"blk": down})
+
+    def w_core(k, half):
         zz = (z + 8 - k) % 8 if k < 4 else (z + k - 3) % 8
-        ref = shard(zz, core)
-        return remote(ref, ref, wcs.at[k], wcr.at[k], {"blk": mate})
-
-    def w_core_in(k):
+        ref = shard(zz, core, half)
+        return remote(ref, ref, wcs.at[k, half], wcr.at[k, half], {"blk": mate})
+
+    def w_core_in(k, half):
         zz = (z + 8 - k) % 8 if k < 4 else (z + k - 3) % 8
-        ref = shard(zz, 1 - core)
-        return remote(ref, ref, wcs.at[k], wcr.at[k], {"blk": mate})
-
-    def w_plus_in(k):
-        ref = shard((z + 7 - k) % 8, core)
-        return remote(ref, ref, wps.at[k], wpr.at[k], {"blk": up})
-
-    def w_minus_in(k):
-        ref = shard((z + 1 + k) % 8, core)
-        return remote(ref, ref, wms.at[k], wmr.at[k], {"blk": down})
+        ref = shard(zz, 1 - core, half)
+        return remote(ref, ref, wcs.at[k, half], wcr.at[k, half], {"blk": mate})
+
+    def w_plus_in(k, half):
+        ref = shard((z + 7 - k) % 8, core, half)
+        return remote(ref, ref, wps.at[k, half], wpr.at[k, half], {"blk": up})
+
+    def w_minus_in(k, half):
+        ref = shard((z + 1 + k) % 8, core, half)
+        return remote(ref, ref, wms.at[k, half], wmr.at[k, half], {"blk": down})
+
+    def w_step_plus(k, half):
+        w_plus_in(k - 1, half).wait_recv()
+        if k < 3:
+            w_plus(k, half).start()
+        w_core(k, half).start()
+
+    def w_step_minus(k, half):
+        w_minus_in(k - 1, half).wait_recv()
+        if k < 4:
+            w_minus(k, half).start()
+        w_core(3 + k, half).start()
 
     loads[3].wait()
-    w_plus(0).start()
-    w_minus(0).start()
+    for half in range(2):
+        w_plus(0, half).start()
+        w_minus(0, half).start()
 
     @pl.loop(1, 16)
     def _(i):
         own_rows(i).start()
 
-    w_core(0).start()
+    for half in range(2):
+        w_core(0, half).start()
 
     loads[0].wait()
     loads[1].wait()
     for n in range(HEADS):
-        at = slice(n * TOKENS, (n + 1) * TOKENS)
-        q_full[at, :LAT] = lax.dot_general(
-            q_raw[n, :NOPE, :], ku[n], (((0,), (0,)), ((), ())), preferred_element_type=F32
+        at = slice(n % 2 * TOKENS, (n % 2 + 1) * TOKENS)
+        q_t[n // 2, :LAT, at] = lax.dot_general(
+            ku[n], q_raw[n, :NOPE, :], (((0,), (0,)), ((), ())), preferred_element_type=F32
         ).astype(BF16)
-        q_full[at, LAT:] = q_raw[n, NOPE:, :].astype(F32).T.astype(BF16)
-
+        q_t[n // 2, LAT:, at] = q_raw[n, NOPE:, :]
+
+    blocks = (
+        (0, c), (1, c), (1, c_mate),
+        (1 - lo, c_side), (1 - lo, c_diag), (2 - 2 * core, c_mate),
+        (2 - lo, c_side), (2 - lo, c_diag),
+    )
     row = lax.broadcasted_iota(jnp.int32, (TOKENS, TOKENS), 0)
     col = lax.broadcasted_iota(jnp.int32, (TOKENS, TOKENS), 1)
-    q_pos = jnp.where(row < HALF, order[2 * b], order[2 * b + 1]) * HALF + row % HALF
-    for n in range(SPAN):
-        src = (b + NBLK - 7 + n) % NBLK
-        k_pos = jnp.where(col < HALF, order[2 * src], order[2 * src + 1]) * HALF + col % HALF
-        bias[:, n * TOKENS:(n + 1) * TOKENS] = jnp.where(k_pos <= q_pos, 0.0, HIDDEN)
+    q_pos = jnp.where(col < HALF, order[2 * b], order[2 * b + 1]) * HALF + col % HALF
+    for j, (plane, cc) in enumerate(blocks):
+        src = (z + 8 - plane) % 8 * 4 + cc
+        k_pos = jnp.where(row < HALF, order[2 * src], order[2 * src + 1]) * HALF + row % HALF
+        bias[j * TOKENS:(j + 1) * TOKENS, :] = jnp.where(k_pos <= q_pos, 0.0, HIDDEN)
+
+    loads[2].wait()
+    for n in range(HEADS):
+        vu_t[n] = vu[n].astype(F32).T.astype(BF16)
 
     @pl.loop(1, 16)
     def _(i):
@@ -196,18 +215,6 @@
         ref = slot(j + 1 - lo, c_diag)
         return remote(ref, ref, lds.at[j], ldr.at[j], {"blk": mate})
 
-    def w_step_plus(k):
-        w_plus_in(k - 1).wait_recv()
-        if k < 3:
-            w_plus(k).start()
-        w_core(k).start()
-
-    def w_step_minus(k):
-        w_minus_in(k - 1).wait_recv()
-        if k < 4:
-            w_minus(k).start()
-        w_core(3 + k).start()
-
     l_up(0, 0).start()
     l_up(0, 1).start()
 
@@ -217,84 +224,133 @@
         l_side(0, 1).start()
 
     l_core(0).start()
-    w_step_minus(1)
+    for half in range(2):
+        w_step_minus(1, half)
+        w_step_plus(1, half)
+
+    def take(j):
+        rows = slot(*blocks[j])[...]
+        near_keys[j * TOKENS:(j + 1) * TOKENS, :] = rows
+        keys_t[:, j * TOKENS:(j + 1) * TOKENS] = rows[:, :LAT].astype(F32).T.astype(BF16)
+
+    take(0)
     for half in range(2):
         l_up_in(0, half).wait_recv()
         l_up(1, half).start()
         l_side(1 - lo, half).start()
 
     l_core(1).start()
-    w_step_plus(1)
-    l_side_in(0, 0).wait_recv()
-    l_side_in(0, 1).wait_recv()
-    l_diag(0).start()
-    for half in range(2):
-        l_up_in(1, half).wait_recv()
-
-        @pl.when(lo == 1)
+    take(1)
+    for half in range(2):
+        w_step_minus(2, half)
+        w_step_plus(2, half)
+    l_core_in(1).wait_recv()
+    take(2)
+
+    def v_out(i):
+        ref = vals.at[lo, pl.ds(pl.multiple_of(i * 256, 256), 256)]
+        return remote(ref, ref, vs.at[i], vr.at[i], {"blk": side})
+
+    def v_in(i):
+        ref = vals.at[1 - lo, pl.ds(pl.multiple_of(i * 256, 256), 256)]
+        return remote(ref, ref, vs.at[i], vr.at[i], {"blk": side})
+
+    def attend(j, first, count, begins, ends):
+        k = near_keys[first:first + count, :]
+        k_t = keys_t[:, first:first + count]
+        for g in range(2):
+            score[g, :count] = jnp.dot(k, q_t[2 * j + g], preferred_element_type=F32)
+        for g in range(2):
+            i = 2 * j + g
+            high = None
+            for r in range(0, count, 64):
+                mask = bias[first + r:first + r + 64, :]
+                sc = score[g, r:r + 64] + jnp.concatenate([mask, mask], axis=1)
+                score[g, r:r + 64] = sc
+                part = jnp.max(sc.reshape(8, 8, 256), axis=0)
+                high = part if high is None else jnp.maximum(high, part)
+            m = jnp.max(high, axis=0, keepdims=True)
+            if not begins:
+                old = top[i, :1]
+                m = jnp.maximum(m, old)
+                shrink = jnp.exp2((old - m) * GAIN)
+            add = None
+            for r in range(0, count, 64):
+                e = jnp.exp2((score[g, r:r + 64] - m) * GAIN)
+                prob[g, r:r + 64] = e.astype(BF16)
+                part = jnp.sum(e.reshape(8, 8, 256), axis=0)
+                add = part if add is None else add + part
+            tot = jnp.sum(add, axis=0, keepdims=True)
+            if not begins:
+                tot = tot + total[i, :1] * shrink
+            if not ends:
+                top[i] = jnp.broadcast_to(m, (8, 256))
+                total[i] = jnp.broadcast_to(tot, (8, 256))
+            got = jnp.dot(k_t, prob[g, :count], preferred_element_type=F32)
+            if begins:
+                accum[i] = got
+            elif not ends:
+                accum[i] = accum[i] * shrink + got
+            else:
+                inverse = 1.0 / tot
+                ctx = (accum[i] * (shrink * inverse) + got * inverse).astype(BF16)
+                for n in range(2):
+                    v = jnp.dot(vu_t[2 * i + n], ctx[:, n * TOKENS:(n + 1) * TOKENS], preferred_element_type=F32)
+                    vals[lo, pl.ds(pl.multiple_of(i * 256 + n * VAL, VAL), VAL), :] = v.astype(BF16)
+                v_out(i).start()
+
+    @pl.loop(0, 2)
+    def _(j):
+        attend(j, 0, 384, True, False)
+
+        @pl.when(j == 0)
         def _():
-            l_side(1, half).start()
-
-    l_core(2).start()
-    w_step_minus(2)
+            l_side_in(0, 0).wait_recv()
+            l_side_in(0, 1).wait_recv()
+            l_diag(0).start()
+            for half in range(2):
+                l_up_in(1, half).wait_recv()
+
+                @pl.when(lo == 1)
+                def _():
+                    l_side(1, half).start()
+
+            l_core(2).start()
+
+    for half in range(2):
+        w_step_minus(3, half)
+    take(3)
+    l_diag_in(0).wait_recv()
+    take(4)
     l_core_in(0).wait_recv()
-    l_core_in(1).wait_recv()
-    l_diag_in(0).wait_recv()
-
-    def scores(i, start, first):
-        q = q_full[pl.ds(pl.multiple_of(i * 256, 256), 256), :]
-        k = keys[pl.ds(pl.multiple_of(start, TOKENS), 512), :]
-        sc = nt_dot(q, k).reshape(2, TOKENS, 512) + bias[:, first:first + 512][None]
-        return sc.reshape(256, 512), k
-
-    def near(i):
-        at = pl.ds(pl.multiple_of(i * 256, 256), 256)
-        sc, k = scores(i, (c + 5) * TOKENS, 512)
-        m = jnp.max(sc, axis=1, keepdims=True)
-        e = jnp.exp2((sc - m) * GAIN)
-        top[at, :] = jnp.broadcast_to(m, (256, 128))
-        total[at, :] = jnp.broadcast_to(jnp.sum(e, axis=1, keepdims=True), (256, 128))
-        accum[at, :] = jnp.dot(e.astype(BF16), k[:, :LAT], preferred_element_type=F32)
-
-    def v_out(i):
-        ref = vals.at[lo, :, pl.ds(pl.multiple_of(i * 256, 256), 256)]
-        return remote(ref, ref, vs.at[i], vr.at[i], {"blk": side})
-
-    def v_in(i):
-        ref = vals.at[1 - lo, :, pl.ds(pl.multiple_of(i * 256, 256), 256)]
-        return remote(ref, ref, vs.at[i], vr.at[i], {"blk": side})
-
-    def far(i):
-        at = pl.ds(pl.multiple_of(i * 256, 256), 256)
-        sc, k = scores(i, (c + 1) * TOKENS, 0)
-        old = top[at, :][:, :1]
-        m = jnp.maximum(old, jnp.max(sc, axis=1, keepdims=True))
-        e = jnp.exp2((sc - m) * GAIN)
-        shrink = jnp.exp2((old - m) * GAIN)
-        tot = total[at, :][:, :1] * shrink + jnp.sum(e, axis=1, keepdims=True)
-        acc = accum[at, :] * shrink + jnp.dot(e.astype(BF16), k[:, :LAT], preferred_element_type=F32)
-        ctx = (acc * (1.0 / tot)).astype(BF16)
-        for n in range(2):
-            v = jnp.dot(ctx[n * TOKENS:(n + 1) * TOKENS], vu[2 * i + n], preferred_element_type=F32)
-            vals[lo, :, pl.ds(pl.multiple_of(i * 256 + n * VAL, VAL), VAL)] = v.astype(BF16)
-        v_out(i).start()
-
-    pl.loop(0, 2)(near)
-    w_step_plus(2)
-    l_side_in(1, 0).wait_recv()
-    l_side_in(1, 1).wait_recv()
-    l_diag(1).start()
-    pl.loop(2, 4)(near)
-    w_step_minus(3)
-    loads[2].wait()
     l_core_in(2).wait_recv()
+    take(5)
+
+    @pl.loop(0, 2)
+    def _(j):
+        attend(j, 384, 384, False, False)
+
+        @pl.when(j == 0)
+        def _():
+            l_side_in(1, 0).wait_recv()
+            l_side_in(1, 1).wait_recv()
+            l_diag(1).start()
+            for half in range(2):
+                w_step_plus(3, half)
+
+    take(6)
+    for half in range(2):
+        w_step_minus(4, half)
     l_diag_in(1).wait_recv()
-    pl.loop(0, 2)(far)
-    w_step_plus(3)
-    pl.loop(2, 4)(far)
-    w_step_minus(4)
+    take(7)
+
+    @pl.loop(0, 2)
+    def _(j):
+        attend(j, 768, 256, False, True)
+
     for k in range(8):
-        w_core_in(k).wait_recv()
+        for half in range(2):
+            w_core_in(k, half).wait_recv()
 
     def x_out(y, n, step, way, kind):
         terms, got, relay = ((terms_a, got_a, relay_a), (terms_b, got_b, relay_b))[n]
@@ -310,7 +366,7 @@
     def project(y, n, step):
         first, width = WIDE[n]
         terms = (terms_a, terms_b)[n]
-        t = nt_dot(vals[y], wt[first:first + 2 * width, :])
+        t = jnp.dot(wt[first:first + 2 * width, :], vals[y], preferred_element_type=F32).T
         left = t[:, :width].reshape(16, 8, width)
         right = t[:, width:].reshape(16, 8, width)
         both = jnp.concatenate([left, right], axis=1).astype(BF16)
@@ -403,12 +459,15 @@
         l_diag(k).wait_send()
     for k in range(3):
         l_core(k).wait_send()
-        w_plus(k).wait_send()
-    for k in range(4):
-        w_minus(k).wait_send()
-        v_out(k).wait_send()
-    for k in range(8):
-        w_core(k).wait_send()
+    for half in range(2):
+        for k in range(3):
+            w_plus(k, half).wait_send()
+        for k in range(4):
+            w_minus(k, half).wait_send()
+        for k in range(8):
+            w_core(k, half).wait_send()
+    for i in range(4):
+        v_out(i).wait_send()
     for n in range(2):
         for way in range(2):
             for kind in range(3):
@@ -424,20 +483,24 @@
     vmem = pl.BlockSpec(memory_space=pltpu.VMEM)
     anywhere = pl.BlockSpec(memory_space=pl.ANY)
     dma = pltpu.SemaphoreType.DMA
-    rows = TOKENS * HEADS
     scratch = [
         pltpu.VMEM((HEADS, NOPE + ROT, TOKENS), BF16),
         pltpu.VMEM((HEADS, NOPE, LAT), BF16),
         pltpu.VMEM((HEADS, LAT, VAL), BF16),
-        pltpu.VMEM((rows, WIDTH), BF16),
-        pltpu.VMEM((TOKENS, SPAN * TOKENS), F32),
+        pltpu.VMEM((HEADS, VAL, LAT), BF16),
+        pltpu.VMEM((4, WIDTH, 256), BF16),
+        pltpu.VMEM((SPAN * TOKENS, TOKENS), F32),
         pltpu.VMEM((16, 16, 384), BF16),
         pltpu.VMEM((12 * TOKENS, WIDTH), BF16),
+        pltpu.VMEM((SPAN * TOKENS, WIDTH), BF16),
+        pltpu.VMEM((LAT, SPAN * TOKENS), BF16),
         pltpu.VMEM((MINE, HEADS * VAL), BF16),
-        pltpu.VMEM((2, TOKENS, HEADS * VAL), BF16),
-        pltpu.VMEM((rows, 128), F32),
-        pltpu.VMEM((rows, 128), F32),
-        pltpu.VMEM((rows, LAT), F32),
+        pltpu.VMEM((2, HEADS * VAL, TOKENS), BF16),
+        pltpu.VMEM((4, 8, 256), F32),
+        pltpu.VMEM((4, 8, 256), F32),
+        pltpu.VMEM((4, LAT, 256), F32),
+        pltpu.VMEM((2, 384, 256), F32),
+        pltpu.VMEM((2, 384, 256), BF16),
         pltpu.VMEM((2, 2, 2, 4, 16, 512), BF16),
         pltpu.VMEM((2, 2, 2, 4, 16, 384), BF16),
         pltpu.VMEM((2, 2, 2, 2, 16, 512), BF16),
@@ -454,9 +517,9 @@
         dma((3,)), dma((3,)),
         dma((2, 2)), dma((2, 2)),
         dma((2,)), dma((2,)),
-        dma((3,)), dma((3,)),
-        dma((4,)), dma((4,)),
-        dma((8,)), dma((8,)),
+        dma((3, 2)), dma((3, 2)),
+        dma((4, 2)), dma((4, 2)),
+        dma((8, 2)), dma((8, 2)),
         dma((4,)), dma((4,)),
         dma((2, 2, 2, 3)), dma((2, 2, 2, 3)),
         dma((2, 4)), dma((2, 4)),

time: 68.6 us -> 70.7 us (1.031)
  the two profiles are of different devices: /device:TPU:1 before, /device:TPU:2 now
where the time goes in v6:
time: 70.7 us; the launch traced here: 70.5 us
  Pallas kernels  69 us (98%)
  local copies, waits for them, and re-layouts  1.45 us (2%)
    pallas_call x1, Pallas kernels, shards(): pl.pallas_call(kernel, out_shape=jax.ShapeDtypeStruct((8, 2 * MINE), BF16...  69 us
    unnamed x1, local copies, waits for them, and re-layouts  1.45 us

profile of v6, /device:TPU:2, one launch (start us, length us, event | category | flops | bytes accessed | tf_op | source)
XLA Modules:
  0.0 70.5 jit_solution(7817541572446161790)
XLA Ops:
  0.0 69.0 %shard_map.64 = bf16[8,3584]{1,0:T(8,128)(2,1)} custom-call(s32[64]{0:T(128)} %order.1, bf16[8,576]{1,0:T(8,128)(2,1)} %latent.1, bf16[8,192,128]{2,1,0:T(8,128)(2,1)} %bitcast.2, bf16[8,128,512]{2,1,0:T(8,128)(2,1)} %ku_hbm.1, bf16[8,512,128]{2,1,0:T(8,128)(2,1)} %vu_hbm.1, bf16[112,1024]{1,0:T(8,128)(2,1)} %bitcast.3), custom_call_target="tpu_custom_call" | custom-call | flops 3500000000 | bytes 3000000 | tf_op jit(solution)/shard_map/pallas_call | solution.py:528
  69.0 1.4 %copy.8 = bf16[8,3584]{1,0:T(8,128)(2,1)} copy(bf16[8,3584]{1,0:T(8,128)(2,1)} %shard_map.64) | data formatting | bytes 114688

commit v7 on v6

--- a/solution.py
+++ b/solution.py
@@ -19,8 +19,7 @@
 SPAN = 8
 NBLK = 32
 COLS = 112
-MINE = 1792
-WIDE = ((0, 512), (1024, 384))
+MINE = 896
 GAIN = (NOPE + ROT) ** (-0.5) * math.log2(math.e)
 HIDDEN = -1e30
 F32 = jnp.float32
@@ -37,9 +36,9 @@
 def kernel(
     order, latent, q_hbm, ku_hbm, vu_hbm, wo_hbm, out,
     q_raw, ku, vu, vu_t, q_t, bias, pack, keys, near_keys, keys_t, wt, vals,
-    top, total, accum, score, prob, terms_a, terms_b, got_a, got_b, relay_a, relay_b, part_a, part_b, fin_a, fin_b,
+    top, total, accum, score, prob, terms, got, relay, part, fin,
     load_sem, ps, pr, lzs, lzr, lcs, lcr, lys, lyr, lds, ldr,
-    wps, wpr, wms, wmr, wcs, wcr, vs, vr, xs, xr, yss, ysr, yos, yor,
+    wps, wpr, wms, wmr, vs, vr, xs, xr, ys, yr,
 ):
     b = lax.axis_index("blk")
     h = lax.axis_index("head")
@@ -50,6 +49,7 @@
     down = (b + NBLK - 4) % NBLK
     mate = b + 1 - 2 * core
     side = b + 2 - 4 * lo
+    diag = side + 1 - 2 * core
     c_mate = c + 1 - 2 * core
     c_side = c + 2 - 4 * lo
     c_diag = c_side + 1 - 2 * core
@@ -58,7 +58,7 @@
         pltpu.make_async_copy(src, dst, load_sem.at[i])
         for i, (src, dst) in enumerate(((q_hbm, q_raw), (ku_hbm, ku), (vu_hbm, vu)))
     ]
-    mine = wt.at[pl.ds(pl.multiple_of((z * 2 + core) * COLS, 16), COLS)]
+    mine = wt.at[pl.ds(pl.multiple_of(z * COLS, 16), COLS)]
     loads.append(pltpu.make_async_copy(wo_hbm, mine, load_sem.at[3]))
     for load in loads[3:] + loads[:3]:
         load.start()
@@ -76,71 +76,59 @@
     def _(i):
         greet({"head": (h + i) % 16})
 
+    for other in (side, diag):
+        @pl.loop(0, 4)
+        def _(i):
+            greet({"blk": other, "head": i * 4 + x})
+
     @pl.loop(0, 4)
     def _(i):
-        greet({"blk": side, "head": (hi + i) % 4 * 4 + x})
+        greet({"blk": mate, "head": i * 4 + x})
 
     greet({"blk": up})
     greet({"blk": down})
-    greet({"blk": mate})
-    pl.semaphore_wait(barrier, 22)
+    pl.semaphore_wait(barrier, 29)
 
     def own_rows(i):
         return remote(pack.at[h], pack.at[h], ps.at[i], pr.at[i], {"head": (h + i) % 16})
 
-    def shard(zz, cc, half):
-        first = (zz * 2 + cc) * COLS + 64 * half
-        return wt.at[pl.ds(pl.multiple_of(first, 16), (64, 48)[half])]
-
-    def w_plus(k, half):
-        ref = shard((z + 8 - k) % 8, core, half)
-        return remote(ref, ref, wps.at[k, half], wpr.at[k, half], {"blk": up})
-
-    def w_minus(k, half):
-        ref = shard((z + k) % 8, core, half)
-        return remote(ref, ref, wms.at[k, half], wmr.at[k, half], {"blk": down})
-
-    def w_core(k, half):
-        zz = (z + 8 - k) % 8 if k < 4 else (z + k - 3) % 8
-        ref = shard(zz, core, half)
-        return remote(ref, ref, wcs.at[k, half], wcr.at[k, half], {"blk": mate})
-
-    def w_core_in(k, half):
-        zz = (z + 8 - k) % 8 if k < 4 else (z + k - 3) % 8
-        ref = shard(zz, 1 - core, half)
-        return remote(ref, ref, wcs.at[k, half], wcr.at[k, half], {"blk": mate})
-
-    def w_plus_in(k, half):
-        ref = shard((z + 7 - k) % 8, core, half)
-        return remote(ref, ref, wps.at[k, half], wpr.at[k, half], {"blk": up})
-
-    def w_minus_in(k, half):
-        ref = shard((z + 1 + k) % 8, core, half)
-        return remote(ref, ref, wms.at[k, half], wmr.at[k, half], {"blk": down})
-
-    def w_step_plus(k, half):
-        w_plus_in(k - 1, half).wait_recv()
+    def shard(zz):
+        return wt.at[pl.ds(pl.multiple_of(zz * COLS, 16), COLS)]
+
+    def w_plus(k):
+        ref = shard((z + 8 - k) % 8)
+        return remote(ref, ref, wps.at[k], wpr.at[k], {"blk": up})
+
+    def w_minus(k):
+        ref = shard((z + k) % 8)
+        return remote(ref, ref, wms.at[k], wmr.at[k], {"blk": down})
+
+    def w_plus_in(k):
+        ref = shard((z + 7 - k) % 8)
+        return remote(ref, ref, wps.at[k], wpr.at[k], {"blk": up})
+
+    def w_minus_in(k):
+        ref = shard((z + 1 + k) % 8)
+        return remote(ref, ref, wms.at[k], wmr.at[k], {"blk": down})
+
+    def w_step_plus(k):
+        w_plus_in(k - 1).wait_recv()
         if k < 3:
-            w_plus(k, half).start()
-        w_core(k, half).start()
-
-    def w_step_minus(k, half):
-        w_minus_in(k - 1, half).wait_recv()
+            w_plus(k).start()
+
+    def w_step_minus(k):
+        w_minus_in(k - 1).wait_recv()
         if k < 4:
-            w_minus(k, half).start()
-        w_core(3 + k, half).start()
+            w_minus(k).start()
 
     loads[3].wait()
-    for half in range(2):
-        w_plus(0, half).start()
-        w_minus(0, half).start()
+    w_plus(0).start()
+    w_minus(0).start()
 
     @pl.loop(1, 16)
     def _(i):
         own_rows(i).start()
 
-    for half in range(2):
-        w_core(0, half).start()
 
     loads[0].wait()
     loads[1].wait()
@@ -224,16 +212,13 @@
         l_side(0, 1).start()
 
     l_core(0).start()
-    for half in range(2):
-        w_step_minus(1, half)
-        w_step_plus(1, half)
-
     def take(j):
         rows = slot(*blocks[j])[...]
         near_keys[j * TOKENS:(j + 1) * TOKENS, :] = rows
         keys_t[:, j * TOKENS:(j + 1) * TOKENS] = rows[:, :LAT].astype(F32).T.astype(BF16)
 
     take(0)
+    w_step_minus(1)
     for half in range(2):
         l_up_in(0, half).wait_recv()
         l_up(1, half).start()
@@ -241,19 +226,37 @@
 
     l_core(1).start()
     take(1)
-    for half in range(2):
-        w_step_minus(2, half)
-        w_step_plus(2, half)
+    w_step_plus(1)
     l_core_in(1).wait_recv()
     take(2)
 
-    def v_out(i):
-        ref = vals.at[lo, pl.ds(pl.multiple_of(i * 256, 256), 256)]
-        return remote(ref, ref, vs.at[i], vr.at[i], {"blk": side})
-
-    def v_in(i):
-        ref = vals.at[1 - lo, pl.ds(pl.multiple_of(i * 256, 256), 256)]
-        return remote(ref, ref, vs.at[i], vr.at[i], {"blk": side})
+    def v_part(y, i, cc):
+        rows = pl.ds(pl.multiple_of(i * 256, 256), 256)
+        return vals.at[y, rows, pl.ds(pl.multiple_of(cc * TOKENS, TOKENS), TOKENS)]
+
+    def v_mate(i):
+        ref = v_part(lo, i, core)
+        return remote(ref, ref, vs.at[0, i], vr.at[0, i], {"blk": mate})
+
+    def v_mate_in(i):
+        ref = v_part(lo, i, 1 - core)
+        return remote(ref, ref, vs.at[0, i], vr.at[0, i], {"blk": mate})
+
+    def v_side(i):
+        ref = v_part(lo, i, core)
+        return remote(ref, ref, vs.at[1, i], vr.at[1, i], {"blk": side})
+
+    def v_side_in(i):
+        ref = v_part(1 - lo, i, core)
+        return remote(ref, ref, vs.at[1, i], vr.at[1, i], {"blk": side})
+
+    def v_diag(i):
+        ref = v_part(1 - lo, i, core)
+        return remote(ref, ref, vs.at[2, i], vr.at[2, i], {"blk": mate})
+
+    def v_diag_in(i):
+        ref = v_part(1 - lo, i, 1 - core)
+        return remote(ref, ref, vs.at[2, i], vr.at[2, i], {"blk": mate})
 
     def attend(j, first, count, begins, ends):
         k = near_keys[first:first + count, :]
@@ -296,8 +299,10 @@
                 ctx = (accum[i] * (shrink * inverse) + got * inverse).astype(BF16)
                 for n in range(2):
                     v = jnp.dot(vu_t[2 * i + n], ctx[:, n * TOKENS:(n + 1) * TOKENS], preferred_element_type=F32)
-                    vals[lo, pl.ds(pl.multiple_of(i * 256 + n * VAL, VAL), VAL), :] = v.astype(BF16)
-                v_out(i).start()
+                    rows = pl.ds(pl.multiple_of(i * 256 + n * VAL, VAL), VAL)
+                    vals[lo, rows, pl.ds(pl.multiple_of(core * TOKENS, TOKENS), TOKENS)] = v.astype(BF16)
+                v_side(i).start()
+                v_mate(i).start()
 
     @pl.loop(0, 2)
     def _(j):
@@ -316,15 +321,15 @@
                     l_side(1, half).start()
 
             l_core(2).start()
-
-    for half in range(2):
-        w_step_minus(3, half)
+            w_step_minus(2)
+
     take(3)
     l_diag_in(0).wait_recv()
     take(4)
     l_core_in(0).wait_recv()
     l_core_in(2).wait_recv()
     take(5)
+    w_step_plus(2)
 
     @pl.loop(0, 2)
     def _(j):
@@ -335,12 +340,9 @@
             l_side_in(1, 0).wait_recv()
             l_side_in(1, 1).wait_recv()
             l_diag(1).start()
-            for half in range(2):
-                w_step_plus(3, half)
+            w_step_minus(3)
 
     take(6)
-    for half in range(2):
-        w_step_minus(4, half)
     l_diag_in(1).wait_recv()
     take(7)
 
@@ -348,104 +350,97 @@
     def _(j):
         attend(j, 768, 256, False, True)
 
-    for k in range(8):
-        for half in range(2):
-            w_core_in(k, half).wait_recv()
+    w_step_plus(3)
+    w_step_minus(4)
 
     def x_out(y, n, step, way, kind):
-        terms, got, relay = ((terms_a, got_a, relay_a), (terms_b, got_b, relay_b))[n]
         xd = (x + 1 + 2 * way) % 4
         if kind == 0:
-            src, dst = terms.at[y, way, :, (x + 2) % 4], relay.at[y, way]
+            src, dst = terms.at[n, y, way, :, (x + 2) % 4], relay.at[n, y, way]
         else:
             half = 1 - way if kind == 1 else way
-            src, dst = terms.at[y, half, :, xd], got.at[y, way, half]
+            src, dst = terms.at[n, y, half, :, xd], got.at[n, y, way, half]
         sem = (n, step, way, kind)
         return remote(src, dst, xs.at[sem], xr.at[sem], {"head": hi * 4 + xd})
 
     def project(y, n, step):
-        first, width = WIDE[n]
-        terms = (terms_a, terms_b)[n]
-        t = jnp.dot(wt[first:first + 2 * width, :], vals[y], preferred_element_type=F32).T
-        left = t[:, :width].reshape(16, 8, width)
-        right = t[:, width:].reshape(16, 8, width)
-        both = jnp.concatenate([left, right], axis=1).astype(BF16)
-        terms[y] = both.reshape(2, 2, 4, 16, width)
+        last = min(MINE, 512 * n + 512)
+        t = jnp.dot(wt[512 * n:last, :], vals[y], preferred_element_type=F32).T
+        if n == 1:
+            t = jnp.concatenate([t, jnp.zeros((256, 128), F32)], axis=1)
+        for cc in range(2):
+            rows = t[cc * TOKENS:(cc + 1) * TOKENS]
+            left = rows[:, :256].reshape(16, 8, 256)
+            right = rows[:, 256:].reshape(16, 8, 256)
+            both = jnp.concatenate([left, right], axis=1).astype(BF16)
+            terms[n, y, :, :, :, cc] = both.reshape(2, 2, 4, 16, 256)
         for kind in range(2):
             for way in range(2):
                 x_out(y, n, step, way, kind).start()
 
     def pass_on(y, n, step):
-        terms, relay = ((terms_a, relay_a), (terms_b, relay_b))[n]
         for way in range(2):
             x_out(y, n, step, way, 0).wait_recv()
             xd = (x + 1 + 2 * way) % 4
-            t = terms[y, way, :, xd].astype(F32) + relay[y, way].astype(F32)
-            terms[y, way, :, xd] = t.astype(BF16)
+            t = terms[n, y, way, :, xd].astype(F32) + relay[n, y, way].astype(F32)
+            terms[n, y, way, :, xd] = t.astype(BF16)
             x_out(y, n, step, way, 2).start()
 
-    def y_same(n, e):
-        part, fin = ((part_a, fin_a), (part_b, fin_b))[n]
-        yd = (hi + e) % 4
-        return remote(
-            part.at[lo, yd], fin.at[0, e], yss.at[n, e], ysr.at[n, e], {"head": yd * 4 + x}
-        )
-
-    def y_other(n, e):
-        part, fin = ((part_a, fin_a), (part_b, fin_b))[n]
-        yd = (hi + e) % 4
-        return remote(
-            part.at[1 - lo, yd], fin.at[1, e], yos.at[n, e], yor.at[n, e],
-            {"blk": side, "head": yd * 4 + x},
-        )
-
     def combine(y, n, step):
-        terms, got, part = ((terms_a, got_a, part_a), (terms_b, got_b, part_b))[n]
-        width = WIDE[n][1]
         for way in range(2):
             x_out(y, n, step, way, 1).wait_recv()
             x_out(y, n, step, way, 2).wait_recv()
-        t = terms[y, :, :, x].astype(F32) + got[y, 0].astype(F32) + got[y, 1].astype(F32)
-        part[y] = t.reshape(4, 16, width).astype(BF16)
-
+        t = terms[n, y, :, :, x].astype(F32) + got[n, y, 0].astype(F32) + got[n, y, 1].astype(F32)
+        part[y, :, :, n] = t.reshape(4, 2, 16, 256).astype(BF16)
+
+    groups = ((b, lo, core), (mate, lo, 1 - core), (side, 1 - lo, core), (diag, 1 - lo, 1 - core))
+
+    def y_out(g, e):
+        blk, y, cc = groups[g]
+        yd = (hi + e) % 4
+        return remote(
+            part.at[y, yd, cc], fin.at[g, e], ys.at[g, e], yr.at[g, e], {"blk": blk, "head": yd * 4 + x}
+        )
+
+    pairs = [(0, e) for e in (2, 1, 3)] + [(g, e) for g in (1, 2, 3) for e in (2, 1, 3, 0)]
+
+    for i in range(4):
+        v_mate_in(i).wait_recv()
     project(lo, 0, 0)
+    for i in range(4):
+        v_side_in(i).wait_recv()
+        v_diag(i).start()
     project(lo, 1, 0)
     pass_on(lo, 0, 0)
     for i in range(4):
-        v_in(i).wait_recv()
+        v_diag_in(i).wait_recv()
     project(1 - lo, 0, 1)
     pass_on(lo, 1, 0)
     project(1 - lo, 1, 1)
     pass_on(1 - lo, 0, 1)
+    combine(lo, 0, 0)
+    combine(lo, 1, 0)
+    for g, e in pairs[:7]:
+        y_out(g, e).start()
     pass_on(1 - lo, 1, 1)
-    for n in range(2):
-        combine(lo, n, 0)
-        for e in (2, 1, 3):
-            y_same(n, e).start()
-    for n in range(2):
-        combine(1 - lo, n, 1)
-        for e in (2, 1, 3, 0):
-            y_other(n, e).start()
-    same_cols, other_cols = [], []
-    for n in range(2):
-        part, fin = ((part_a, fin_a), (part_b, fin_b))[n]
-        same = part[lo, hi].astype(F32)
-        for e in (1, 2, 3):
-            y_same(n, e).wait_recv()
-            same = same + fin[0, e].astype(F32)
-        y_other(n, 0).wait_recv()
-        other = fin[1, 0].astype(F32)
-        for e in (1, 2, 3):
-            y_other(n, e).wait_recv()
-            other = other + fin[1, e].astype(F32)
-        same_cols += [same[:8], same[8:]]
-        other_cols += [other[:8], other[8:]]
-    same = jnp.concatenate(same_cols, axis=1)
-    other = jnp.concatenate(other_cols, axis=1)
-    by_y = (jnp.where(lo == 0, same, other), jnp.where(lo == 0, other, same))
-    pair = 2 * COLS
+    combine(1 - lo, 0, 1)
+    combine(1 - lo, 1, 1)
+    for g, e in pairs[7:]:
+        y_out(g, e).start()
+    sums = [part[lo, hi, core].astype(F32), None, None, None]
+    for g, e in pairs:
+        y_out(g, e).wait_recv()
+        v = fin[g, e].astype(F32)
+        sums[g] = v if sums[g] is None else sums[g] + v
+    flat = [
+        jnp.concatenate([v[0, :8], v[0, 8:], v[1, :8], v[1, 8:, :128]], axis=1) for v in sums
+    ]
+    by_c = [
+        jnp.where(c == a, flat[0], jnp.where(c_mate == a, flat[1], jnp.where(c_side == a, flat[2], flat[3])))
+        for a in range(4)
+    ]
     out[...] = jnp.concatenate(
-        [by_y[i % 2][:, i // 2 * pair:(i // 2 + 1) * pair] for i in range(16)], axis=1
+        [by_c[i % 4][:, i // 4 * COLS:(i // 4 + 1) * COLS] for i in range(NBLK)], axis=1
     ).astype(BF16)
 
     @pl.loop(1, 16)
@@ -459,24 +454,21 @@
         l_diag(k).wait_send()
     for k in range(3):
         l_core(k).wait_send()
-    for half in range(2):
-        for k in range(3):
-            w_plus(k, half).wait_send()
-        for k in range(4):
-            w_minus(k, half).wait_send()
-        for k in range(8):
-            w_core(k, half).wait_send()
+    for k in range(3):
+        w_plus(k).wait_send()
+    for k in range(4):
+        w_minus(k).wait_send()
     for i in range(4):
-        v_out(i).wait_send()
+        v_side(i).wait_send()
+        v_mate(i).wait_send()
+        v_diag(i).wait_send()
     for n in range(2):
         for way in range(2):
             for kind in range(3):
                 x_out(lo, n, 0, way, kind).wait_send()
                 x_out(1 - lo, n, 1, way, kind).wait_send()
-        for e in (1, 2, 3):
-            y_same(n, e).wait_send()
-        for e in range(4):
-            y_other(n, e).wait_send()
+    for g, e in pairs:
+        y_out(g, e).wait_send()
 
 
 def shards(queries, latent, key_up_weight, value_up_weight, w_o, block_order):
@@ -495,39 +487,32 @@
         pltpu.VMEM((SPAN * TOKENS, WIDTH), BF16),
         pltpu.VMEM((LAT, SPAN * TOKENS), BF16),
         pltpu.VMEM((MINE, HEADS * VAL), BF16),
-        pltpu.VMEM((2, HEADS * VAL, TOKENS), BF16),
+        pltpu.VMEM((2, HEADS * VAL, 2 * TOKENS), BF16),
         pltpu.VMEM((4, 8, 256), F32),
         pltpu.VMEM((4, 8, 256), F32),
         pltpu.VMEM((4, LAT, 256), F32),
         pltpu.VMEM((2, 384, 256), F32),
         pltpu.VMEM((2, 384, 256), BF16),
-        pltpu.VMEM((2, 2, 2, 4, 16, 512), BF16),
-        pltpu.VMEM((2, 2, 2, 4, 16, 384), BF16),
-        pltpu.VMEM((2, 2, 2, 2, 16, 512), BF16),
-        pltpu.VMEM((2, 2, 2, 2, 16, 384), BF16),
-        pltpu.VMEM((2, 2, 2, 16, 512), BF16),
-        pltpu.VMEM((2, 2, 2, 16, 384), BF16),
-        pltpu.VMEM((2, 4, 16, 512), BF16),
-        pltpu.VMEM((2, 4, 16, 384), BF16),
-        pltpu.VMEM((2, 4, 16, 512), BF16),
-        pltpu.VMEM((2, 4, 16, 384), BF16),
+        pltpu.VMEM((2, 2, 2, 2, 4, 2, 16, 256), BF16),
+        pltpu.VMEM((2, 2, 2, 2, 2, 2, 16, 256), BF16),
+        pltpu.VMEM((2, 2, 2, 2, 2, 16, 256), BF16),
+        pltpu.VMEM((2, 4, 2, 2, 16, 256), BF16),
+        pltpu.VMEM((4, 4, 2, 16, 256), BF16),
         dma((4,)),
         dma((16,)), dma((16,)),
         dma((2, 2)), dma((2, 2)),
         dma((3,)), dma((3,)),
         dma((2, 2)), dma((2, 2)),
         dma((2,)), dma((2,)),
-        dma((3, 2)), dma((3, 2)),
-        dma((4, 2)), dma((4, 2)),
-        dma((8, 2)), dma((8, 2)),
+        dma((3,)), dma((3,)),
         dma((4,)), dma((4,)),
+        dma((3, 4)), dma((3, 4)),
         dma((2, 2, 2, 3)), dma((2, 2, 2, 3)),
-        dma((2, 4)), dma((2, 4)),
-        dma((2, 4)), dma((2, 4)),
+        dma((4, 4)), dma((4, 4)),
     ]
     return pl.pallas_call(
         kernel,
-        out_shape=jax.ShapeDtypeStruct((8, 2 * MINE), BF16),
+        out_shape=jax.ShapeDtypeStruct((8, NBLK * COLS), BF16),
         in_specs=[pl.BlockSpec(memory_space=pltpu.SMEM), vmem] + [anywhere] * 4,
         out_specs=vmem,
         scratch_shapes=scratch,

time: 70.7 us -> 71 us (level)
  the two profiles are of different devices: /device:TPU:2 before, /device:TPU:1 now
where the time goes in v7:
time: 71 us; the launch traced here: 70.8 us
  Pallas kernels  69.4 us (98%)
  local copies, waits for them, and re-layouts  1.45 us (2%)
    pallas_call x1, Pallas kernels, shards(): pl.pallas_call(kernel, out_shape=jax.ShapeDtypeStruct((8, NBLK * COLS), B...  69.4 us
    unnamed x1, local copies, waits for them, and re-layouts  1.45 us

profile of v7, /device:TPU:1, one launch (start us, length us, event | category | flops | bytes accessed | tf_op | source)
XLA Modules:
  0.0 70.8 jit_solution(6098442711281102502)
XLA Ops:
  0.0 69.4 %shard_map.64 = bf16[8,3584]{1,0:T(8,128)(2,1)} custom-call(s32[64]{0:T(128)} %order.1, bf16[8,576]{1,0:T(8,128)(2,1)} %latent.1, bf16[8,192,128]{2,1,0:T(8,128)(2,1)} %bitcast.2, bf16[8,128,512]{2,1,0:T(8,128)(2,1)} %ku_hbm.1, bf16[8,512,128]{2,1,0:T(8,128)(2,1)} %vu_hbm.1, bf16[112,1024]{1,0:T(8,128)(2,1)} %bitcast.3), custom_call_target="tpu_custom_call" | custom-call | flops 3500000000 | bytes 3000000 | tf_op jit(solution)/shard_map/pallas_call | solution.py:513
  69.4 1.4 %copy.8 = bf16[8,3584]{1,0:T(8,128)(2,1)} copy(bf16[8,3584]{1,0:T(8,128)(2,1)} %shard_map.64) | data formatting | bytes 114688

commit v8 on v4

--- a/solution.py
+++ b/solution.py
@@ -12,6 +12,7 @@
 ROT = 64
 LAT = 512
 WIDTH = LAT + ROT
+PADDED = 640
 VAL = 128
 HEADS = 8
 TOKENS = 128
@@ -167,7 +168,7 @@
     gathered = pack[...].astype(F32)
     base = pl.multiple_of((8 + c) * TOKENS, TOKENS)
     keys[pl.ds(base, TOKENS), :384] = gathered[:, :8, :].reshape(TOKENS, 384).astype(BF16)
-    keys[pl.ds(base, TOKENS), 384:] = gathered[:, 8:, :192].reshape(TOKENS, 192).astype(BF16)
+    keys[pl.ds(base, TOKENS), 384:] = gathered[:, 8:, :256].reshape(TOKENS, 256).astype(BF16)
 
     def l_up(k, half):
         src, dst = part_slot(k, c, half), part_slot(k + 1, c, half)
@@ -256,7 +257,7 @@
         return pl.ds(pl.multiple_of(t * 512 + g * 256 + first, 32), count)
 
     def step(t, start, first, last):
-        k = keys[pl.ds(pl.multiple_of(start, TOKENS), 512), :]
+        k = keys[pl.ds(pl.multiple_of(start, TOKENS), 512), :WIDTH]
         for g in range(2):
             score[g] = nt_dot(q_full[rows_at(t, g, 0, 256), :], k)
         for g in range(2):
@@ -461,7 +462,7 @@
         pltpu.VMEM((rows, WIDTH), BF16),
         pltpu.VMEM((TOKENS, SPAN * TOKENS), F32),
         pltpu.VMEM((16, 16, 384), BF16),
-        pltpu.VMEM((12 * TOKENS, WIDTH), BF16),
+        pltpu.VMEM((12 * TOKENS, PADDED), BF16),
         pltpu.VMEM((MINE, HEADS * VAL), BF16),
         pltpu.VMEM((2, 2, HALF, HEADS * VAL), BF16),
         pltpu.VMEM((rows, 128), F32),

time: 67.5 us -> 67.5 us (level)
  no operation moved by 1% of the time
where the time goes in v8:
time: 67.5 us; the launch traced here: 67.3 us
  Pallas kernels  65.9 us (98%)
  local copies, waits for them, and re-layouts  1.45 us (2%)
    pallas_call x1, Pallas kernels, shards(): pl.pallas_call(kernel, out_shape=jax.ShapeDtypeStruct((8, 2 * MINE), BF16...  65.9 us
    unnamed x1, local copies, waits for them, and re-layouts  1.45 us

profile of v8, /device:TPU:56, one launch (start us, length us, event | category | flops | bytes accessed | tf_op | source)
XLA Modules:
  0.0 67.3 jit_solution(15519622316927692839)
XLA Ops:
  0.0 65.9 %shard_map.64 = bf16[8,3584]{1,0:T(8,128)(2,1)} custom-call(s32[64]{0:T(128)} %order.1, bf16[8,576]{1,0:T(8,128)(2,1)} %latent.1, bf16[8,192,128]{2,1,0:T(8,128)(2,1)} %bitcast.2, bf16[8,128,512]{2,1,0:T(8,128)(2,1)} %ku_hbm.1, bf16[8,512,128]{2,1,0:T(8,128)(2,1)} %vu_hbm.1, bf16[112,1024]{1,0:T(8,128)(2,1)} %bitcast.3), custom_call_target="tpu_custom_call" | custom-call | flops 3500000000 | bytes 3000000 | tf_op jit(solution)/shard_map/pallas_call | solution.py:498
  65.9 1.4 %copy.8 = bf16[8,3584]{1,0:T(8,128)(2,1)} copy(bf16[8,3584]{1,0:T(8,128)(2,1)} %shard_map.64) | data formatting | bytes 114688

commit v9 on v4

--- a/solution.py
+++ b/solution.py
@@ -40,8 +40,8 @@
 
 
 def kernel(
-    order, latent, q_hbm, ku_hbm, vu_hbm, wo_hbm, out,
-    q_raw, ku, vu, q_full, bias, pack, keys, wt, vals,
+    order_hbm, latent_hbm, q_hbm, ku_hbm, vu_hbm, wo_hbm, out,
+    order, latent, q_raw, ku, vu, q_full, bias, pack, keys, wt, vals,
     top, total, accum, score, prob, ctx, terms_a, terms_b, got_a, got_b, relay_a, relay_b, part_a, part_b, fin_a, fin_b,
     load_sem, ps, pr, lzs, lzr, lcs, lcr, lys, lyr, lds, ldr,
     wps, wpr, wms, wmr, wcs, wcr, vs, vr, xs, xr, yss, ysr, yos, yor,
@@ -55,6 +55,7 @@
     down = (b + NBLK - 4) % NBLK
     mate = b + 1 - 2 * core
     side = b + 2 - 4 * lo
+    up_side, down_side = (side + 4) % NBLK, (side + NBLK - 4) % NBLK
     c_mate = c + 1 - 2 * core
     c_side = c + 2 - 4 * lo
     c_diag = c_side + 1 - 2 * core
@@ -65,30 +66,34 @@
     ]
     mine = wt.at[pl.ds(pl.multiple_of((z * 2 + core) * COLS, 16), COLS)]
     loads.append(pltpu.make_async_copy(wo_hbm, mine, load_sem.at[3]))
-    for load in loads[3:] + loads[:3]:
+    loads.append(pltpu.make_async_copy(latent_hbm, latent, load_sem.at[4]))
+    loads.append(pltpu.make_async_copy(order_hbm, order, load_sem.at[5]))
+    for load in loads[4:] + loads[3:4] + loads[:3]:
         load.start()
 
+    barrier = pltpu.get_barrier_semaphore()
+
+    def greet(device):
+        pl.semaphore_signal(barrier, inc=1, device_id=device, device_id_type=pl.DeviceIdType.MESH)
+
+    @pl.loop(1, 16)
+    def _(i):
+        greet({"head": (h + i) % 16})
+
+    @pl.loop(0, 4)
+    def _(i):
+        greet({"blk": side, "head": (hi + i) % 4 * 4 + x})
+
+    greet({"blk": up})
+    greet({"blk": down})
+    greet({"blk": mate})
+    greet({"blk": up_side})
+    greet({"blk": down_side})
+    loads[4].wait()
     rows = latent[...].astype(F32)
     second = jnp.concatenate([rows[:, 384:], jnp.zeros((8, 192), F32)], axis=1)
     pack[h] = jnp.concatenate([rows[:, :384], second], axis=0).astype(BF16)
-
-    barrier = pltpu.get_barrier_semaphore()
-
-    def greet(device):
-        pl.semaphore_signal(barrier, inc=1, device_id=device, device_id_type=pl.DeviceIdType.MESH)
-
-    @pl.loop(1, 16)
-    def _(i):
-        greet({"head": (h + i) % 16})
-
-    @pl.loop(0, 4)
-    def _(i):
-        greet({"blk": side, "head": (hi + i) % 4 * 4 + x})
-
-    greet({"blk": up})
-    greet({"blk": down})
-    greet({"blk": mate})
-    pl.semaphore_wait(barrier, 22)
+    pl.semaphore_wait(barrier, 24)
 
     def own_rows(i):
         return remote(pack.at[h], pack.at[h], ps.at[i], pr.at[i], {"head": (h + i) % 16})
@@ -144,6 +149,7 @@
             q_full[at, :LAT] = lat[t * HALF:(t + 1) * HALF]
             q_full[at, LAT:] = turned[t * HALF:(t + 1) * HALF]
 
+    loads[5].wait()
     row = lax.broadcasted_iota(jnp.int32, (TOKENS, TOKENS), 0)
     col = lax.broadcasted_iota(jnp.int32, (TOKENS, TOKENS), 1)
     q_pos = jnp.where(row < HALF, order[2 * b], order[2 * b + 1]) * HALF + row % HALF
@@ -184,8 +190,10 @@
         return remote(slot(p, c_mate), slot(p, c_mate), lcs.at[p], lcr.at[p], {"blk": mate})
 
     def l_side(j, half):
-        ref = part_slot(j + lo, c, half)
-        return remote(ref, ref, lys.at[j, half], lyr.at[j, half], {"blk": side})
+        src = part_slot(j * lo, c, half)
+        dst = part_slot(j + lo, c, half)
+        blk = side * (1 - lo) + up_side * lo if j == 0 else up_side
+        return remote(src, dst, lys.at[j, half], lyr.at[j, half], {"blk": blk})
 
     def l_side_in(j, half):
         ref = part_slot(j + 1 - lo, c_side, half)
@@ -214,17 +222,23 @@
     l_up(0, 0).start()
     l_up(0, 1).start()
 
+    l_side(0, 0).start()
+    l_side(0, 1).start()
+
     @pl.when(lo == 0)
     def _():
-        l_side(0, 0).start()
-        l_side(0, 1).start()
+        l_side(1, 0).start()
+        l_side(1, 1).start()
 
     l_core(0).start()
     w_step_minus(1)
     for half in range(2):
         l_up_in(0, half).wait_recv()
         l_up(1, half).start()
-        l_side(1 - lo, half).start()
+
+        @pl.when(lo == 1)
+        def _():
+            l_side(1, half).start()
 
     l_core(1).start()
     w_step_plus(1)
@@ -233,10 +247,6 @@
     l_diag(0).start()
     for half in range(2):
         l_up_in(1, half).wait_recv()
-
-        @pl.when(lo == 1)
-        def _():
-            l_side(1, half).start()
 
     l_core(2).start()
     w_step_minus(2)
@@ -455,6 +465,8 @@
     dma = pltpu.SemaphoreType.DMA
     rows = TOKENS * HEADS
     scratch = [
+        pltpu.SMEM((64,), jnp.int32),
+        pltpu.VMEM((8, WIDTH), BF16),
         pltpu.VMEM((HEADS, NOPE + ROT, TOKENS), BF16),
         pltpu.VMEM((HEADS, NOPE, LAT), BF16),
         pltpu.VMEM((HEADS, LAT, VAL), BF16),
@@ -480,7 +492,7 @@
         pltpu.VMEM((4, 2, 16, 384), BF16),
         pltpu.VMEM((2, 4, 16, 512), BF16),
         pltpu.VMEM((2, 4, 16, 384), BF16),
-        dma((4,)),
+        dma((6,)),
         dma((16,)), dma((16,)),
         dma((2, 2)), dma((2, 2)),
         dma((3,)), dma((3,)),
@@ -497,7 +509,7 @@
     return pl.pallas_call(
         kernel,
         out_shape=jax.ShapeDtypeStruct((8, 2 * MINE), BF16),
-        in_specs=[pl.BlockSpec(memory_space=pltpu.SMEM), vmem] + [anywhere] * 4,
+        in_specs=[anywhere] * 6,
         out_specs=vmem,
         scratch_shapes=scratch,
         compiler_params=pltpu.CompilerParams(

time: 67.5 us -> 71.7 us (1.062)
  Pallas kernels: 65.9 us -> 70.1 us
    pallas_call x1, Pallas kernels: 65.9 us -> 70.1 us  [shards(): pl.pallas_call(kernel, out_shape=jax.ShapeDtypeStruct((8, 2 * MINE), BF16...]
where the time goes in v9:
time: 71.7 us; the launch traced here: 71.5 us
  Pallas kernels  70.1 us (98%)
  local copies, waits for them, and re-layouts  1.45 us (2%)
    pallas_call x1, Pallas kernels, shards(): pl.pallas_call(kernel, out_shape=jax.ShapeDtypeStruct((8, 2 * MINE), BF16...  70.1 us
    unnamed x1, local copies, waits for them, and re-layouts  1.45 us

profile of v9, /device:TPU:56, one launch (start us, length us, event | category | flops | bytes accessed | tf_op | source)
XLA Modules:
  0.0 71.5 jit_solution(5470778820349902771)
XLA Ops:
  0.0 70.1 %shard_map.64 = bf16[8,3584]{1,0:T(8,128)(2,1)} custom-call(s32[64]{0:T(128)} %order_hbm.1, bf16[8,576]{1,0:T(8,128)(2,1)} %latent_hbm.1, bf16[8,192,128]{2,1,0:T(8,128)(2,1)} %bitcast.2, bf16[8,128,512]{2,1,0:T(8,128)(2,1)} %ku_hbm.1, bf16[8,512,128]{2,1,0:T(8,128)(2,1)} %vu_hbm.1, bf16[112,1024]{1,0:T(8,128)(2,1)} %bitcast.3), custom_call_target="tpu_custom_call" | custom-call | flops 3500000000 | bytes 3000000 | tf_op jit(solution)/shard_map/pallas_call | solution.py:509
  70.1 1.4 %copy.8 = bf16[8,3584]{1,0:T(8,128)(2,1)} copy(bf16[8,3584]{1,0:T(8,128)(2,1)} %shard_map.64) | data formatting | bytes 114688

commit v10 on v5

--- a/solution.py
+++ b/solution.py
@@ -225,16 +225,16 @@
     l_core(0).start()
     for half in range(2):
         w_step_minus(1, half)
-        w_step_plus(1, half)
     for half in range(2):
         l_up_in(0, half).wait_recv()
         l_up(1, half).start()
         l_side(1 - lo, half).start()
 
     l_core(1).start()
-    for half in range(2):
-        w_step_minus(2, half)
-        w_step_plus(2, half)
+    w_step_minus(2, 0)
+    for half in range(2):
+        w_step_plus(1, half)
+    w_step_minus(2, 1)
     l_side_in(0, 0).wait_recv()
     l_side_in(0, 1).wait_recv()
     l_diag(0).start()
@@ -246,8 +246,6 @@
             l_side(1, half).start()
 
     l_core(2).start()
-    for half in range(2):
-        w_step_minus(3, half)
     l_core_in(0).wait_recv()
     l_core_in(1).wait_recv()
     l_diag_in(0).wait_recv()
@@ -311,9 +309,11 @@
             l_side_in(1, 0).wait_recv()
             l_side_in(1, 1).wait_recv()
             l_diag(1).start()
-
-    for half in range(2):
-        w_step_plus(3, half)
+            for half in range(2):
+                w_step_minus(3, half)
+            for half in range(2):
+                w_step_plus(2, half)
+
     loads[2].wait()
     l_core_in(2).wait_recv()
     l_diag_in(1).wait_recv()
@@ -326,8 +326,10 @@
         @pl.when(t == 0)
         def _():
             for half in range(2):
-                w_step_minus(4, half)
-
+                w_step_plus(3, half)
+
+    for half in range(2):
+        w_step_minus(4, half)
     for k in range(8):
         for half in range(2):
             w_core_in(k, half).wait_recv()

time: 70.3 us -> 66.6 us (0.947)
  Pallas kernels: 68.6 us -> 64.9 us
    pallas_call x1, Pallas kernels: 68.6 us -> 64.9 us  [shards(): pl.pallas_call(kernel, out_shape=jax.ShapeDtypeStruct((8, 2 * MINE), BF16...]
where the time goes in v10:
time: 66.6 us; the launch traced here: 66.4 us
  Pallas kernels  64.9 us (97%)
  local copies, waits for them, and re-layouts  1.45 us (2%)
    pallas_call x1, Pallas kernels, shards(): pl.pallas_call(kernel, out_shape=jax.ShapeDtypeStruct((8, 2 * MINE), BF16...  64.9 us
    unnamed x1, local copies, waits for them, and re-layouts  1.45 us

profile of v10, /device:TPU:56, one launch (start us, length us, event | category | flops | bytes accessed | tf_op | source)
XLA Modules:
  0.0 66.4 jit_solution(14268508385256417415)
XLA Ops:
  0.0 64.9 %shard_map.64 = bf16[8,3584]{1,0:T(8,128)(2,1)} custom-call(s32[64]{0:T(128)} %order.1, bf16[8,576]{1,0:T(8,128)(2,1)} %latent.1, bf16[8,192,128]{2,1,0:T(8,128)(2,1)} %bitcast.2, bf16[8,128,512]{2,1,0:T(8,128)(2,1)} %ku_hbm.1, bf16[8,512,128]{2,1,0:T(8,128)(2,1)} %vu_hbm.1, bf16[112,1024]{1,0:T(8,128)(2,1)} %bitcast.3), custom_call_target="tpu_custom_call" | custom-call | flops 3500000000 | bytes 3000000 | tf_op jit(solution)/shard_map/pallas_call | solution.py:510
  65.0 1.4 %copy.8 = bf16[8,3584]{1,0:T(8,128)(2,1)} copy(bf16[8,3584]{1,0:T(8,128)(2,1)} %shard_map.64) | data formatting | bytes 114688

commit v11 on v10

--- a/solution.py
+++ b/solution.py
@@ -21,6 +21,9 @@
 COLS = 112
 MINE = 1792
 WIDE = ((0, 512), (1024, 384))
+BELOW = (0, 1, 3, 6)
+ABOVE = (0, 2, 4, 5, 7)
+OFFSET = (0, 7, 1, 6, 2, 3, 5, 4)
 GAIN = (NOPE + ROT) ** (-0.5) * math.log2(math.e)
 HIDDEN = -1e30
 NT = (((1,), (1,)), ((), ()))
@@ -63,7 +66,7 @@
         pltpu.make_async_copy(src, dst, load_sem.at[i])
         for i, (src, dst) in enumerate(((q_hbm, q_raw), (ku_hbm, ku), (vu_hbm, vu)))
     ]
-    mine = wt.at[pl.ds(pl.multiple_of((z * 2 + core) * COLS, 16), COLS)]
+    mine = wt.at[pl.ds(pl.multiple_of(core * COLS, 16), COLS)]
     loads.append(pltpu.make_async_copy(wo_hbm, mine, load_sem.at[3]))
     for load in loads[3:] + loads[:3]:
         load.start()
@@ -93,34 +96,32 @@
     def own_rows(i):
         return remote(pack.at[h], pack.at[h], ps.at[i], pr.at[i], {"head": (h + i) % 16})
 
-    def shard(zz, cc, half):
-        first = (zz * 2 + cc) * COLS + 64 * half
+    def shard(place, cc, half):
+        first = (place * 2 + cc) * COLS + 64 * half
         return wt.at[pl.ds(pl.multiple_of(first, 16), (64, 48)[half])]
 
     def w_plus(k, half):
-        ref = shard((z + 8 - k) % 8, core, half)
+        src, dst = shard(BELOW[k], core, half), shard(BELOW[k + 1], core, half)
+        return remote(src, dst, wps.at[k, half], wpr.at[k, half], {"blk": up})
+
+    def w_minus(k, half):
+        src, dst = shard(ABOVE[k], core, half), shard(ABOVE[k + 1], core, half)
+        return remote(src, dst, wms.at[k, half], wmr.at[k, half], {"blk": down})
+
+    def w_core(k, half):
+        ref = shard(BELOW[k] if k < 4 else ABOVE[k - 3], core, half)
+        return remote(ref, ref, wcs.at[k, half], wcr.at[k, half], {"blk": mate})
+
+    def w_core_in(k, half):
+        ref = shard(BELOW[k] if k < 4 else ABOVE[k - 3], 1 - core, half)
+        return remote(ref, ref, wcs.at[k, half], wcr.at[k, half], {"blk": mate})
+
+    def w_plus_in(k, half):
+        ref = shard(BELOW[k + 1], core, half)
         return remote(ref, ref, wps.at[k, half], wpr.at[k, half], {"blk": up})
 
-    def w_minus(k, half):
-        ref = shard((z + k) % 8, core, half)
-        return remote(ref, ref, wms.at[k, half], wmr.at[k, half], {"blk": down})
-
-    def w_core(k, half):
-        zz = (z + 8 - k) % 8 if k < 4 else (z + k - 3) % 8
-        ref = shard(zz, core, half)
-        return remote(ref, ref, wcs.at[k, half], wcr.at[k, half], {"blk": mate})
-
-    def w_core_in(k, half):
-        zz = (z + 8 - k) % 8 if k < 4 else (z + k - 3) % 8
-        ref = shard(zz, 1 - core, half)
-        return remote(ref, ref, wcs.at[k, half], wcr.at[k, half], {"blk": mate})
-
-    def w_plus_in(k, half):
-        ref = shard((z + 7 - k) % 8, core, half)
-        return remote(ref, ref, wps.at[k, half], wpr.at[k, half], {"blk": up})
-
     def w_minus_in(k, half):
-        ref = shard((z + 1 + k) % 8, core, half)
+        ref = shard(ABOVE[k + 1], core, half)
         return remote(ref, ref, wms.at[k, half], wmr.at[k, half], {"blk": down})
 
     def w_step_plus(k, half):
@@ -323,17 +324,6 @@
         step(t, (c + 1) * TOKENS, 0, True)
         v_out(t).start()
 
-        @pl.when(t == 0)
-        def _():
-            for half in range(2):
-                w_step_plus(3, half)
-
-    for half in range(2):
-        w_step_minus(4, half)
-    for k in range(8):
-        for half in range(2):
-            w_core_in(k, half).wait_recv()
-
     def x_out(t, n, way, kind):
         terms, got, relay = ((terms_a, got_a, relay_a), (terms_b, got_b, relay_b))[n]
         xd = (x + 1 + 2 * way) % 4
@@ -395,19 +385,29 @@
             def _():
                 y_same(n, yd, hi).start()
 
+    def w_ready(ks):
+        for k in ks:
+            for half in range(2):
+                w_core_in(k, half).wait_recv()
+
+    w_ready((0, 1, 2, 4, 5))
     v_in(0).wait_recv()
     project(0, 0)
-    project(0, 1)
-    pass_on(0, 0)
+    for half in range(2):
+        w_step_plus(3, half)
+        w_step_minus(4, half)
     v_in(1).wait_recv()
     project(1, 0)
-    pass_on(0, 1)
+    pass_on(0, 0)
+    w_ready((3, 6, 7))
+    project(0, 1)
+    pass_on(1, 0)
     project(1, 1)
     combine(0, 0)
-    pass_on(1, 0)
+    pass_on(0, 1)
+    combine(1, 0)
+    pass_on(1, 1)
     combine(0, 1)
-    pass_on(1, 1)
-    combine(1, 0)
     combine(1, 1)
     same_cols, other_cols = [], []
     for n in range(2):
@@ -427,9 +427,14 @@
     other = jnp.concatenate(other_cols, axis=1)
     by_y = (jnp.where(lo == 0, same, other), jnp.where(lo == 0, other, same))
     pair = 2 * COLS
-    out[...] = jnp.concatenate(
-        [by_y[i % 2][:, i // 2 * pair:(i // 2 + 1) * pair] for i in range(16)], axis=1
-    ).astype(BF16)
+    pieces = []
+    for i in range(16):
+        places = [by_y[i % 2][:, n * pair:(n + 1) * pair] for n in range(8)]
+        piece = places[0]
+        for n in range(1, 8):
+            piece = jnp.where((z + OFFSET[n]) % 8 == i // 2, places[n], piece)
+        pieces.append(piece)
+    out[...] = jnp.concatenate(pieces, axis=1).astype(BF16)
 
     @pl.loop(1, 16)
     def _(i):

time: 66.6 us -> 67.8 us (1.018)
  Pallas kernels: 64.9 us -> 66.1 us
    pallas_call x1, Pallas kernels: 64.9 us -> 66.1 us  [shards(): pl.pallas_call(kernel, out_shape=jax.ShapeDtypeStruct((8, 2 * MINE), BF16...]
where the time goes in v11:
time: 67.8 us; the launch traced here: 67.6 us
  Pallas kernels  66.1 us (97%)
  local copies, waits for them, and re-layouts  1.45 us (2%)
    pallas_call x1, Pallas kernels, shards(): pl.pallas_call(kernel, out_shape=jax.ShapeDtypeStruct((8, 2 * MINE), BF16...  66.1 us
    unnamed x1, local copies, waits for them, and re-layouts  1.45 us

profile of v11, /device:TPU:56, one launch (start us, length us, event | category | flops | bytes accessed | tf_op | source)
XLA Modules:
  0.0 67.6 jit_solution(10393774671434066111)
XLA Ops:
  0.0 66.1 %shard_map.64 = bf16[8,3584]{1,0:T(8,128)(2,1)} custom-call(s32[64]{0:T(128)} %order.1, bf16[8,576]{1,0:T(8,128)(2,1)} %latent.1, bf16[8,192,128]{2,1,0:T(8,128)(2,1)} %bitcast.2, bf16[8,128,512]{2,1,0:T(8,128)(2,1)} %ku_hbm.1, bf16[8,512,128]{2,1,0:T(8,128)(2,1)} %vu_hbm.1, bf16[112,1024]{1,0:T(8,128)(2,1)} %bitcast.3), custom_call_target="tpu_custom_call" | custom-call | flops 3500000000 | bytes 3000000 | tf_op jit(solution)/shard_map/pallas_call | solution.py:515
  66.1 1.4 %copy.8 = bf16[8,3584]{1,0:T(8,128)(2,1)} copy(bf16[8,3584]{1,0:T(8,128)(2,1)} %shard_map.64) | data formatting | bytes 114688

commit v12 on v10

--- a/solution.py
+++ b/solution.py
@@ -40,8 +40,8 @@
 
 
 def kernel(
-    order, latent, q_hbm, ku_hbm, vu_hbm, wo_hbm, out,
-    q_raw, ku, vu, q_full, bias, pack, keys, wt, vals,
+    order_hbm, latent_hbm, q_hbm, ku_hbm, vu_hbm, wo_hbm, out,
+    order, latent, q_raw, ku, vu, q_full, bias, pack, keys, wt, vals,
     top, total, accum, score, prob, ctx, terms_a, terms_b, got_a, got_b, relay_a, relay_b, part_a, part_b, fin_a, fin_b,
     load_sem, ps, pr, lzs, lzr, lcs, lcr, lys, lyr, lds, ldr,
     wps, wpr, wms, wmr, wcs, wcr, vs, vr, xs, xr, yss, ysr, yos, yor,
@@ -65,33 +65,40 @@
     ]
     mine = wt.at[pl.ds(pl.multiple_of((z * 2 + core) * COLS, 16), COLS)]
     loads.append(pltpu.make_async_copy(wo_hbm, mine, load_sem.at[3]))
-    for load in loads[3:] + loads[:3]:
+    loads.append(pltpu.make_async_copy(latent_hbm, latent, load_sem.at[4]))
+    loads.append(pltpu.make_async_copy(order_hbm, order, load_sem.at[5]))
+    loads[4].start()
+
+    barrier = pltpu.get_barrier_semaphore()
+
+    def greet(device):
+        pl.semaphore_signal(barrier, inc=1, device_id=device, device_id_type=pl.DeviceIdType.MESH)
+
+    @pl.loop(1, 16)
+    def _(i):
+        greet({"head": (h + i) % 16})
+
+    @pl.loop(0, 4)
+    def _(i):
+        greet({"blk": side, "head": (hi + i) % 4 * 4 + x})
+
+    greet({"blk": up})
+    greet({"blk": down})
+    greet({"blk": mate})
+    for load in loads[3:4] + loads[:3] + loads[5:]:
         load.start()
-
+    loads[4].wait()
     rows = latent[...].astype(F32)
     second = jnp.concatenate([rows[:, 384:], jnp.zeros((8, 192), F32)], axis=1)
     pack[h] = jnp.concatenate([rows[:, :384], second], axis=0).astype(BF16)
-
-    barrier = pltpu.get_barrier_semaphore()
-
-    def greet(device):
-        pl.semaphore_signal(barrier, inc=1, device_id=device, device_id_type=pl.DeviceIdType.MESH)
+    pl.semaphore_wait(barrier, 22)
+
+    def own_rows(i):
+        return remote(pack.at[h], pack.at[h], ps.at[i], pr.at[i], {"head": (h + i) % 16})
 
     @pl.loop(1, 16)
     def _(i):
-        greet({"head": (h + i) % 16})
-
-    @pl.loop(0, 4)
-    def _(i):
-        greet({"blk": side, "head": (hi + i) % 4 * 4 + x})
-
-    greet({"blk": up})
-    greet({"blk": down})
-    greet({"blk": mate})
-    pl.semaphore_wait(barrier, 22)
-
-    def own_rows(i):
-        return remote(pack.at[h], pack.at[h], ps.at[i], pr.at[i], {"head": (h + i) % 16})
+        own_rows(i).start()
 
     def shard(zz, cc, half):
         first = (zz * 2 + cc) * COLS + 64 * half
@@ -139,10 +146,6 @@
     for half in range(2):
         w_plus(0, half).start()
         w_minus(0, half).start()
-
-    @pl.loop(1, 16)
-    def _(i):
-        own_rows(i).start()
 
     for half in range(2):
         w_core(0, half).start()
@@ -159,6 +162,7 @@
             q_full[at, :LAT] = lat[t * HALF:(t + 1) * HALF]
             q_full[at, LAT:] = turned[t * HALF:(t + 1) * HALF]
 
+    loads[5].wait()
     row = lax.broadcasted_iota(jnp.int32, (TOKENS, TOKENS), 0)
     col = lax.broadcasted_iota(jnp.int32, (TOKENS, TOKENS), 1)
     q_pos = jnp.where(row < HALF, order[2 * b], order[2 * b + 1]) * HALF + row % HALF
@@ -468,6 +472,8 @@
     dma = pltpu.SemaphoreType.DMA
     rows = TOKENS * HEADS
     scratch = [
+        pltpu.SMEM((64,), jnp.int32),
+        pltpu.VMEM((8, WIDTH), BF16),
         pltpu.VMEM((HEADS, NOPE + ROT, TOKENS), BF16),
         pltpu.VMEM((HEADS, NOPE, LAT), BF16),
         pltpu.VMEM((HEADS, LAT, VAL), BF16),
@@ -493,7 +499,7 @@
         pltpu.VMEM((4, 2, 16, 384), BF16),
         pltpu.VMEM((2, 4, 16, 512), BF16),
         pltpu.VMEM((2, 4, 16, 384), BF16),
-        dma((4,)),
+        dma((6,)),
         dma((16,)), dma((16,)),
         dma((2, 2)), dma((2, 2)),
         dma((3,)), dma((3,)),
@@ -510,7 +516,7 @@
     return pl.pallas_call(
         kernel,
         out_shape=jax.ShapeDtypeStruct((8, 2 * MINE), BF16),
-        in_specs=[pl.BlockSpec(memory_space=pltpu.SMEM), vmem] + [anywhere] * 4,
+        in_specs=[anywhere] * 6,
         out_specs=vmem,
         scratch_shapes=scratch,
         compiler_params=pltpu.CompilerParams(

time: 66.6 us -> 65.9 us (0.989)
  no operation moved by 1% of the time
where the time goes in v12:
time: 65.9 us; the launch traced here: 65.7 us
  Pallas kernels  64.3 us (98%)
  local copies, waits for them, and re-layouts  1.45 us (2%)
    pallas_call x1, Pallas kernels, shards(): pl.pallas_call(kernel, out_shape=jax.ShapeDtypeStruct((8, 2 * MINE), BF16...  64.3 us
    unnamed x1, local copies, waits for them, and re-layouts  1.45 us

profile of v12, /device:TPU:56, one launch (start us, length us, event | category | flops | bytes accessed | tf_op | source)
XLA Modules:
  0.0 65.7 jit_solution(9551951450614280423)
XLA Ops:
  0.0 64.3 %shard_map.64 = bf16[8,3584]{1,0:T(8,128)(2,1)} custom-call(s32[64]{0:T(128)} %order_hbm.1, bf16[8,576]{1,0:T(8,128)(2,1)} %latent_hbm.1, bf16[8,192,128]{2,1,0:T(8,128)(2,1)} %bitcast.2, bf16[8,128,512]{2,1,0:T(8,128)(2,1)} %ku_hbm.1, bf16[8,512,128]{2,1,0:T(8,128)(2,1)} %vu_hbm.1, bf16[112,1024]{1,0:T(8,128)(2,1)} %bitcast.3), custom_call_target="tpu_custom_call" | custom-call | flops 3500000000 | bytes 3000000 | tf_op jit(solution)/shard_map/pallas_call | solution.py:516
  64.3 1.4 %copy.8 = bf16[8,3584]{1,0:T(8,128)(2,1)} copy(bf16[8,3584]{1,0:T(8,128)(2,1)} %shard_map.64) | data formatting | bytes 114688

commit v13 on v12

--- a/solution.py
+++ b/solution.py
@@ -42,7 +42,7 @@
 def kernel(
     order_hbm, latent_hbm, q_hbm, ku_hbm, vu_hbm, wo_hbm, out,
     order, latent, q_raw, ku, vu, q_full, bias, pack, keys, wt, vals,
-    top, total, accum, score, prob, ctx, terms_a, terms_b, got_a, got_b, relay_a, relay_b, part_a, part_b, fin_a, fin_b,
+    top, total, accum, score, prob, ctx, terms_a, terms_b, got_a, got_b, part_a, part_b, fin_a, fin_b,
     load_sem, ps, pr, lzs, lzr, lcs, lcr, lys, lyr, lds, ldr,
     wps, wpr, wms, wmr, wcs, wcr, vs, vr, xs, xr, yss, ysr, yos, yor,
 ):
@@ -338,16 +338,13 @@
         for half in range(2):
             w_core_in(k, half).wait_recv()
 
-    def x_out(t, n, way, kind):
-        terms, got, relay = ((terms_a, got_a, relay_a), (terms_b, got_b, relay_b))[n]
-        xd = (x + 1 + 2 * way) % 4
-        if kind == 0:
-            src, dst = terms.at[t, way, (x + 2) % 4], relay.at[t, way]
-        else:
-            r = 1 - way if kind == 1 else way
-            src, dst = terms.at[t, r, xd], got.at[t, way, r]
-        sem = (t, n, way, kind)
-        return remote(src, dst, xs.at[sem], xr.at[sem], {"head": hi * 4 + xd})
+    def x_out(t, n, d):
+        terms, got = ((terms_a, got_a), (terms_b, got_b))[n]
+        xd = (x + d) % 4
+        return remote(
+            terms.at[t, :, xd], got.at[t, d - 1],
+            xs.at[t, n, d - 1], xr.at[t, n, d - 1], {"head": hi * 4 + xd},
+        )
 
     def project(t, n):
         first, width = WIDE[n]
@@ -359,18 +356,8 @@
             right = out[y * HALF:(y + 1) * HALF, width:].reshape(8, 8, width)
             pair = jnp.concatenate([left, right], axis=1).astype(BF16)
             terms[t, :, :, y] = pair.reshape(2, 4, 16, width)
-        for kind in range(2):
-            for way in range(2):
-                x_out(t, n, way, kind).start()
-
-    def pass_on(t, n):
-        terms, relay = ((terms_a, relay_a), (terms_b, relay_b))[n]
-        for way in range(2):
-            x_out(t, n, way, 0).wait_recv()
-            xd = (x + 1 + 2 * way) % 4
-            both = terms[t, way, xd].astype(F32) + relay[t, way].astype(F32)
-            terms[t, way, xd] = both.astype(BF16)
-            x_out(t, n, way, 2).start()
+        for d in (2, 1, 3):
+            x_out(t, n, d).start()
 
     def y_same(n, yd, src):
         part, fin = ((part_a, fin_a), (part_b, fin_b))[n]
@@ -387,10 +374,10 @@
 
     def combine(t, n):
         terms, got, part = ((terms_a, got_a, part_a), (terms_b, got_b, part_b))[n]
-        for way in range(2):
-            x_out(t, n, way, 1).wait_recv()
-            x_out(t, n, way, 2).wait_recv()
-        both = terms[t, :, x].astype(F32) + got[t, 0].astype(F32) + got[t, 1].astype(F32)
+        both = terms[t, :, x].astype(F32)
+        for d in (1, 3, 2):
+            x_out(t, n, d).wait_recv()
+            both = both + got[t, d - 1].astype(F32)
         part[2 * t:2 * t + 2] = both.astype(BF16)
         for yd in (2 * t, 2 * t + 1):
             y_other(n, yd, hi).start()
@@ -402,15 +389,11 @@
     v_in(0).wait_recv()
     project(0, 0)
     project(0, 1)
-    pass_on(0, 0)
     v_in(1).wait_recv()
     project(1, 0)
-    pass_on(0, 1)
     project(1, 1)
     combine(0, 0)
-    pass_on(1, 0)
     combine(0, 1)
-    pass_on(1, 1)
     combine(1, 0)
     combine(1, 1)
     same_cols, other_cols = [], []
@@ -457,9 +440,8 @@
         v_out(t).wait_send()
     for n in range(2):
         for t in range(2):
-            for way in range(2):
-                for kind in range(3):
-                    x_out(t, n, way, kind).wait_send()
+            for d in (1, 2, 3):
+                x_out(t, n, d).wait_send()
         for yd in range(4):
             y_other(n, yd, hi).wait_send()
         for e in (1, 2, 3):
@@ -491,10 +473,8 @@
         pltpu.VMEM((2, 256, LAT), BF16),
         pltpu.VMEM((2, 2, 4, 2, 16, 512), BF16),
         pltpu.VMEM((2, 2, 4, 2, 16, 384), BF16),
-        pltpu.VMEM((2, 2, 2, 2, 16, 512), BF16),
-        pltpu.VMEM((2, 2, 2, 2, 16, 384), BF16),
-        pltpu.VMEM((2, 2, 2, 16, 512), BF16),
-        pltpu.VMEM((2, 2, 2, 16, 384), BF16),
+        pltpu.VMEM((2, 3, 2, 2, 16, 512), BF16),
+        pltpu.VMEM((2, 3, 2, 2, 16, 384), BF16),
         pltpu.VMEM((4, 2, 16, 512), BF16),
         pltpu.VMEM((4, 2, 16, 384), BF16),
         pltpu.VMEM((2, 4, 16, 512), BF16),
@@ -509,7 +489,7 @@
         dma((4, 2)), dma((4, 2)),
         dma((8, 2)), dma((8, 2)),
         dma((2,)), dma((2,)),
-        dma((2, 2, 2, 3)), dma((2, 2, 2, 3)),
+        dma((2, 2, 3)), dma((2, 2, 3)),
         dma((2, 4)), dma((2, 4)),
         dma((2, 4)), dma((2, 4)),
     ]

time: 65.9 us -> 66.4 us (level)
  no operation moved by 1% of the time
where the time goes in v13:
time: 66.4 us; the launch traced here: 65.7 us
  Pallas kernels  64.2 us (97%)
  local copies, waits for them, and re-layouts  1.45 us (2%)
    pallas_call x1, Pallas kernels, shards(): pl.pallas_call(kernel, out_shape=jax.ShapeDtypeStruct((8, 2 * MINE), BF16...  64.2 us
    unnamed x1, local copies, waits for them, and re-layouts  1.45 us

profile of v13, /device:TPU:56, one launch (start us, length us, event | category | flops | bytes accessed | tf_op | source)
XLA Modules:
  0.0 65.7 jit_solution(11951446376721894192)
XLA Ops:
  0.0 64.2 %shard_map.64 = bf16[8,3584]{1,0:T(8,128)(2,1)} custom-call(s32[64]{0:T(128)} %order_hbm.1, bf16[8,576]{1,0:T(8,128)(2,1)} %latent_hbm.1, bf16[8,192,128]{2,1,0:T(8,128)(2,1)} %bitcast.2, bf16[8,128,512]{2,1,0:T(8,128)(2,1)} %ku_hbm.1, bf16[8,512,128]{2,1,0:T(8,128)(2,1)} %vu_hbm.1, bf16[112,1024]{1,0:T(8,128)(2,1)} %bitcast.3), custom_call_target="tpu_custom_call" | custom-call | flops 3500000000 | bytes 3000000 | tf_op jit(solution)/shard_map/pallas_call | solution.py:496
  64.2 1.4 %copy.8 = bf16[8,3584]{1,0:T(8,128)(2,1)} copy(bf16[8,3584]{1,0:T(8,128)(2,1)} %shard_map.64) | data formatting | bytes 114688

commit v14 on v12

--- a/solution.py
+++ b/solution.py
@@ -236,8 +236,6 @@
 
     l_core(1).start()
     w_step_minus(2, 0)
-    for half in range(2):
-        w_step_plus(1, half)
     w_step_minus(2, 1)
     l_side_in(0, 0).wait_recv()
     l_side_in(0, 1).wait_recv()
@@ -250,6 +248,8 @@
             l_side(1, half).start()
 
     l_core(2).start()
+    for half in range(2):
+        w_step_plus(1, half)
     l_core_in(0).wait_recv()
     l_core_in(1).wait_recv()
     l_diag_in(0).wait_recv()
@@ -315,9 +315,9 @@
             l_diag(1).start()
             for half in range(2):
                 w_step_minus(3, half)
-            for half in range(2):
-                w_step_plus(2, half)
-
+
+    for half in range(2):
+        w_step_plus(2, half)
     loads[2].wait()
     l_core_in(2).wait_recv()
     l_diag_in(1).wait_recv()
@@ -327,13 +327,10 @@
         step(t, (c + 1) * TOKENS, 0, True)
         v_out(t).start()
 
-        @pl.when(t == 0)
-        def _():
-            for half in range(2):
-                w_step_plus(3, half)
-
     for half in range(2):
         w_step_minus(4, half)
+    for half in range(2):
+        w_step_plus(3, half)
     for k in range(8):
         for half in range(2):
             w_core_in(k, half).wait_recv()

time: 65.9 us -> 66.8 us (1.014)
  Pallas kernels: 64.3 us -> 65.1 us
    pallas_call x1, Pallas kernels: 64.3 us -> 65.1 us  [shards(): pl.pallas_call(kernel, out_shape=jax.ShapeDtypeStruct((8, 2 * MINE), BF16...]
where the time goes in v14:
time: 66.8 us; the launch traced here: 66.6 us
  Pallas kernels  65.1 us (97%)
  local copies, waits for them, and re-layouts  1.45 us (2%)
    pallas_call x1, Pallas kernels, shards(): pl.pallas_call(kernel, out_shape=jax.ShapeDtypeStruct((8, 2 * MINE), BF16...  65.1 us
    unnamed x1, local copies, waits for them, and re-layouts  1.45 us

profile of v14, /device:TPU:56, one launch (start us, length us, event | category | flops | bytes accessed | tf_op | source)
XLA Modules:
  0.0 66.6 jit_solution(14000945419420127822)
XLA Ops:
  0.0 65.1 %shard_map.64 = bf16[8,3584]{1,0:T(8,128)(2,1)} custom-call(s32[64]{0:T(128)} %order_hbm.1, bf16[8,576]{1,0:T(8,128)(2,1)} %latent_hbm.1, bf16[8,192,128]{2,1,0:T(8,128)(2,1)} %bitcast.2, bf16[8,128,512]{2,1,0:T(8,128)(2,1)} %ku_hbm.1, bf16[8,512,128]{2,1,0:T(8,128)(2,1)} %vu_hbm.1, bf16[112,1024]{1,0:T(8,128)(2,1)} %bitcast.3), custom_call_target="tpu_custom_call" | custom-call | flops 3500000000 | bytes 3000000 | tf_op jit(solution)/shard_map/pallas_call | solution.py:513
  65.1 1.4 %copy.8 = bf16[8,3584]{1,0:T(8,128)(2,1)} copy(bf16[8,3584]{1,0:T(8,128)(2,1)} %shard_map.64) | data formatting | bytes 114688
